TPU v7x, 256 devices: a whole 4x4x8 slice. The times are simulated.
256 devices in a mesh: leaf: 64 (over z, y, core), front: 4 (over x).
Axes of the slice: x: 4, y: 4, z: 8, core: 2. Of those that a mesh axis runs over, the one named last changes fastest.
Arguments:
- front: bfloat16 [64, 2, 4, 256, 2048], P('leaf', None, 'front')
- pivot_tiles: int32 [64], P('leaf'), may hold values from 1 to 2, as said below
- send_table: int32 [64, 4, 3, 64], P('leaf', 'front'), may hold values from -1 to 15, as said below
Outputs:
- factor: float32 [64, 2, 4, 256, 512], P('leaf', None, 'front')
- ancestor: float32 [64, 4, 16, 256, 256], P('leaf', 'front')
Inputs may be any that keep to these rules, and one draw needn't show every extreme that they name: Front s eliminates its first pivot_tiles[s] tile columns; some front has 2 and some has 1. `send_table`: slot p of device (s, g) goes to leaf p. A slot is either unused (all three entries -1) or names a local tile row r and tile column j whose global tile row r * 4 + g and column j are both at least pivot_tiles[s], with an ancestor slot; every such tile of the device is named by exactly one slot. The 1 slots to leaf 0 are used on every device.
All inputs are finite; a program needn't handle non-finite values.
Results may differ from a plain program's by a relative error of at most 0.0003.
Values sent between devices are 32-bit elements; how exact they have to be, the bound alone decides.
No kernel may reach another device: no remote copies, remote signals or barrier semaphores. Data moves between devices by JAX's collectives and lax.ppermute only.
A program may use at most 128 MiB of HBM per device.

v0:
```python
import jax
import jax.numpy as jnp
from jax import lax
from jax.sharding import PartitionSpec as P

PT = 2
ASLOT = 16


highest = lax.Precision.HIGHEST


def solve_panel(diagonal, panel_rows):
    factor_tile = jnp.linalg.cholesky(diagonal)
    return lax.linalg.triangular_solve(
        factor_tile, panel_rows, left_side=False, lower=True, transpose_a=True
    )


def local(front, pivot_tiles, send_table):
    row_tiles = front.shape[1]
    tile = front.shape[3]
    width = front.shape[4]
    grid = lax.axis_size("front")
    place = lax.axis_index("front")
    col_tiles = width // tile
    own_rows = row_tiles * tile
    pivot_width = PT * tile
    pivots = pivot_tiles[0]
    work = front[0, :, 0].astype(jnp.float32).reshape(own_rows, width)
    columns = []
    all_tiles = jnp.arange(width, dtype=jnp.int32) // tile
    for panel in range(PT):
        left = panel * tile
        piece = lax.slice_in_dim(work, left, left + tile, axis=1).reshape(row_tiles, 1, tile, tile)
        whole = lax.all_gather(piece, "front", axis=1, tiled=True).reshape(width, tile)
        diagonal = lax.slice_in_dim(whole, left, left + tile, axis=0)
        solved = solve_panel(diagonal, whole)
        keep = (all_tiles >= panel) & (panel < pivots)
        solved = jnp.where(keep[:, None], solved, 0.0)
        mine = lax.dynamic_index_in_dim(
            solved.reshape(row_tiles, grid, tile, tile), place, 1, keepdims=False
        )
        mine = mine.reshape(own_rows, tile)
        work = work - jnp.dot(mine, solved.T, precision=highest)
        columns.append(mine)
    factor = jnp.concatenate(columns, axis=1)
    tiles_all = work.reshape(row_tiles, tile, col_tiles, tile).transpose(0, 2, 1, 3)
    tiles_all = tiles_all.reshape(row_tiles * col_tiles, tile * tile)
    table = send_table[0, 0]
    live = table[0] >= 0
    position = jnp.clip(table[0] * col_tiles + table[1], 0, row_tiles * col_tiles - 1)
    outgoing = jnp.where(live[:, None], jnp.take(tiles_all, position, axis=0), 0.0)
    arrived, targets = (
        lax.all_to_all(outgoing, "leaf", split_axis=0, concat_axis=0, tiled=True),
        lax.all_to_all(table[2], "leaf", split_axis=0, concat_axis=0, tiled=True),
    )
    onehot = (targets[:, None] == jnp.arange(ASLOT, dtype=jnp.int32)[None, :]).astype(jnp.float32)
    ancestor = jnp.dot(onehot.T, arrived, precision=highest).reshape(1, 1, ASLOT, tile, tile)
    return (factor.reshape(1, row_tiles, 1, tile, pivot_width), ancestor)


def solution(mesh):
    in_specs = (P("leaf", None, "front", None, None), P("leaf"), P("leaf", "front", None, None))
    out_specs = (P("leaf", None, "front", None, None), P("leaf", "front", None, None, None))
    return jax.shard_map(local, mesh=mesh, in_specs=in_specs, out_specs=out_specs, check_vma=False)
```

profile of v0, /device:TPU:49, one launch (start us, length us, event | category | flops | bytes accessed | tf_op | source)
XLA Modules:
  0.0 713.6 jit_solution(5560120464656257594)
XLA Ops:
  7.2 2.1 bitcast_convert_fusion
  9.3 2.0 copy-done.1
  12.9 35.2 %all-gather.3.cloned.1.call-done = f32[2,4,256,256]{3,2,0,1:T(8,128)} async-done(((f32[2,1,256,256]{3,2,0,1:T(8,128)}), f32[2,4,256,256]{3,2,0,1:T(8,128)}) %all-gather.3.cloned.1.call-update) | async-done | bytes 2097168 | tf_op jit(solution)/shard_map/all_gather | solution.py:36
  48.1 3.0 copy.32
  51.2 2.3 reshape.208
  53.8 11.7 %cholesky.130 = f32[128,128]{1,0:T(8,128)S(1)} custom-call(f32[128,128]{1,0:T(8,128)S(1)} %cholesky.194), custom_call_target="Cholesky" | custom-call | tf_op jit(solution)/shard_map/jit(cholesky)/cholesky | solution.py:14
  65.5 9.8 %custom-call.13 = f32[1,128,128]{1,2,0:T(8,128)S(1)} custom-call(f32[1,128,128]{2,1,0:T(8,128)S(1)} %get-tuple-element.61), custom_call_target="InvertDiagBlocksLowerTriangular" | custom-call | tf_op jit(solution)/shard_map/jit(cholesky)/cholesky | solution.py:14
  75.8 11.7 %cholesky.147 = f32[128,128]{1,0:T(8,128)S(1)} custom-call(f32[128,128]{1,0:T(8,128)S(1)} %convolution_subtract_fusion.5), custom_call_target="Cholesky" | custom-call | tf_op jit(solution)/shard_map/jit(cholesky)/cholesky | solution.py:14
  89.8 4.1 while.4
  90.4 1.4 bitcast_dynamic-update-slice_fusion.4
  92.4 1.4 bitcast_dynamic-update-slice_fusion.4
  93.9 20.1 %custom-call.14 = f32[2,128,128]{1,2,0:T(8,128)S(1)} custom-call(f32[2,128,128]{2,1,0:T(8,128)S(1)} %get-tuple-element.18), custom_call_target="InvertDiagBlocksLowerTriangular" | custom-call | tf_op jit(solution)/shard_map/triangular_solve/custom-call.0 | solution.py:15
  114.0 1.1 fusion.9
  115.1 1.1 convolution_subtract_fusion.3
  116.2 1.1 fusion.17
  117.4 2.5 reshape.209
  119.9 3.5 fusion.35
  123.4 5.5 convolution_subtract_fusion.1
  128.9 2.0 copy-done
  131.0 0.8 slice.107
  132.5 11.0 %all-to-all-start = ((s32[64,1,1]{2,1,0:T(1,128)}), s32[64,1,1]{2,1,0:T(1,128)S(1)}, u32[]{:S(2)}, u32[]{:S(2)}) async-start(s32[64,1,1]{2,1,0:T(1,128)} %copy.40), calls=%async_computation | async-start | bytes 65536 | tf_op jit(solution)/shard_map/all_to_all | solution.py:56
  143.7 21.7 %all-gather.5.cloned.1.call-done = f32[2,4,256,256]{3,2,0,1:T(8,128)} async-done(((f32[2,1,256,256]{3,2,0,1:T(8,128)}), f32[2,4,256,256]{3,2,0,1:T(8,128)}) %all-gather.5.cloned.1.call-update) | async-done | bytes 2097168 | tf_op jit(solution)/shard_map/all_gather | solution.py:36
  165.4 3.0 copy.36
  168.4 2.3 reshape.212
  171.0 11.7 %cholesky.164 = f32[128,128]{1,0:T(8,128)S(1)} custom-call(f32[128,128]{1,0:T(8,128)S(1)} %cholesky.197), custom_call_target="Cholesky" | custom-call | tf_op jit(solution)/shard_map/jit(cholesky)/cholesky | solution.py:14
  182.8 9.8 %custom-call.15 = f32[1,128,128]{1,2,0:T(8,128)S(1)} custom-call(f32[1,128,128]{2,1,0:T(8,128)S(1)} %get-tuple-element.57), custom_call_target="InvertDiagBlocksLowerTriangular" | custom-call | tf_op jit(solution)/shard_map/jit(cholesky)/cholesky | solution.py:14
  193.1 11.7 %cholesky.181 = f32[128,128]{1,0:T(8,128)S(1)} custom-call(f32[128,128]{1,0:T(8,128)S(1)} %convolution_subtract_fusion.4), custom_call_target="Cholesky" | custom-call | tf_op jit(solution)/shard_map/jit(cholesky)/cholesky | solution.py:14
  207.6 4.1 while.5
  208.2 1.4 bitcast_dynamic-update-slice_fusion.5
  210.3 1.4 bitcast_dynamic-update-slice_fusion.5
  211.7 19.9 %custom-call.16 = f32[2,128,128]{1,2,0:T(8,128)S(1)} custom-call(f32[2,128,128]{2,1,0:T(8,128)S(1)} %get-tuple-element.19), custom_call_target="InvertDiagBlocksLowerTriangular" | custom-call | tf_op jit(solution)/shard_map/triangular_solve/custom-call.0 | solution.py:15
  231.6 1.1 fusion.7
  232.6 1.1 convolution_subtract_fusion.2
  233.7 1.1 fusion.13
  235.0 2.5 reshape.213
  237.5 3.5 fusion.34
  241.0 5.8 convolution_subtract_fusion
  246.8 4.0 copy.50
  250.8 20.2 %gather_fusion = f32[64,65536]{1,0:T(8,128)} fusion(f32[16,65536]{1,0:T(8,128)} %bitcast.128, s32[1024]{0:T(1024)S(1)} %pad_clamp_fusion), kind=kCustom, calls=%fused_computation | custom fusion | bytes 33554688 | tf_op jit(solution)/shard_map/jit(_take)/gather | solution.py:53
  271.0 6.8 fusion.3
  277.8 20.2 %copy.41 = f32[64,1,65536]{2,1,0:T(1,128)} copy(f32[64,1,65536]{2,0,1:T(8,128)S(1)} %fusion.3) | data formatting | bytes 33554432 | tf_op jit(solution)/shard_map/jit(_where)/select_n | solution.py:53
  298.0 11.0 %all-to-all-start.1 = ((f32[64,1,65536]{2,1,0:T(1,128)}), f32[64,1,65536]{2,1,0:T(1,128)}, u32[]{:S(2)}, u32[]{:S(2)}) async-start(f32[64,1,65536]{2,1,0:T(1,128)} %copy.41), calls=%async_computation.1 | async-start | bytes 33554432 | tf_op jit(solution)/shard_map/all_to_all | solution.py:55
  309.0 1.2 reduce.9
  311.2 1.1 pad_maximum_fusion
  312.3 368.6 %all-to-all-done.1 = f32[64,1,65536]{2,1,0:T(1,128)} async-done(((f32[64,1,65536]{2,1,0:T(1,128)}), f32[64,1,65536]{2,1,0:T(1,128)}, u32[]{:S(2)}, u32[]{:S(2)}) %all-to-all-start.1) | async-done | bytes 16777248 | tf_op jit(solution)/shard_map/all_to_all | solution.py:55
  681.0 15.4 %copy.46 = f32[64,1,65536]{2,0,1:T(8,128)S(1)} copy(f32[64,1,65536]{2,1,0:T(1,128)} %all-to-all-done.1) | data formatting | bytes 33554432
  696.4 5.6 fusion.4
  702.1 4.4 copy.43
  (59 shorter events, 9.2 us)
Async XLA Ops:
  7.2 41.0 %all-gather.3.cloned.1.call-start = ((), (), s32[]{:S(2)}) async-start(), calls=%async_computation.2 | async-start | bytes 2621440 | tf_op jit(solution)/shard_map/all_gather | solution.py:36
  9.3 2.0 copy-start.1
  12.2 153.2 %all-gather.5.cloned.1.call-start = ((), (), s32[]{:S(2)}) async-start(), calls=%async_computation.3 | async-start | bytes 2621440 | tf_op jit(solution)/shard_map/all_gather | solution.py:36
  123.4 8.4 %copy-start.2 = (s32[1,1,3,64]{3,1,2,0:T(1,128)S(1)}, s32[1,1,3,64]{3,1,2,0:T(1,128)}, u32[]{:S(2)}) copy-start(s32[1,1,3,64]{3,1,2,0:T(1,128)} %param.8) | copy-start | bytes 2308
  128.9 2.0 copy-start
  132.5 165.5 %all-to-all-start = ((s32[64,1,1]{2,1,0:T(1,128)}), s32[64,1,1]{2,1,0:T(1,128)S(1)}, u32[]{:S(2)}, u32[]{:S(2)}) async-start(s32[64,1,1]{2,1,0:T(1,128)} %copy.40), calls=%async_computation | async-start | bytes 65536 | tf_op jit(solution)/shard_map/all_to_all | solution.py:56
  298.0 383.0 %all-to-all-start.1 = ((f32[64,1,65536]{2,1,0:T(1,128)}), f32[64,1,65536]{2,1,0:T(1,128)}, u32[]{:S(2)}, u32[]{:S(2)}) async-start(f32[64,1,65536]{2,1,0:T(1,128)} %copy.41), calls=%async_computation.1 | async-start | bytes 33554432 | tf_op jit(solution)/shard_map/all_to_all | solution.py:55
Sparse Core Ops, SparseCore 0:
  12.3 35.7 all-gather.2
  131.9 33.4 all-gather.4
where the time goes:
time: 723 us; the launch traced here: 714 us
  waiting for transfers between devices  426 us (59%)
  other arithmetic  120 us (17%)
  local copies, waits for them, and re-layouts  103 us (14%)
  matrix products  24.3 us (3%)
  starting transfers between devices  22.1 us (3%)
  between operations  18 us (2%)
    all_to_all x1, waiting for transfers between devices, local(): lax.all_to_all(outgoing, 'leaf', split_axis=0, concat_axis=0, tiled=True)  369 us
    another operation x13, other arithmetic, solve_panel(): factor_tile = jnp.linalg.cholesky(diagonal)  68.7 us
    all_gather x2, waiting for transfers between devices, local(): lax.all_gather(piece, 'front', axis=1, tiled=True).reshape(width, tile)  57 us
    another operation x5, other arithmetic, solve_panel(): lax.linalg.triangular_solve(factor_tile, panel_rows, left_side=False, low...  40.1 us
    unnamed x11, local copies, waits for them, and re-layouts  27.9 us
    select_n x1, local copies, waits for them, and re-layouts, local(): jnp.where(live[:, None], jnp.take(tiles_all, position, axis=0), 0.0)  20.2 us
    gather x1, local copies, waits for them, and re-layouts, local(): jnp.take(tiles_all, position, axis=0)  20.2 us
  transfers between devices with their start and end apart: 4, of which 3 were waited for; matrix products, arithmetic and copies ran while one was open for 19% of the time, Pallas kernels for 0%

commit v1 on v0

v1 whole, which is shorter than its diff:
```python
import functools

import jax
import jax.numpy as jnp
from jax import lax
from jax.experimental import pallas as pl
from jax.experimental.pallas import tpu as pltpu
from jax.sharding import PartitionSpec as P

PT = 2
ASLOT = 16
B = 64
T = 256
F32 = jnp.float32
BF16 = jnp.bfloat16
HIGHEST = lax.Precision.HIGHEST
VMEM = pl.BlockSpec(memory_space=pltpu.VMEM)
SMEM = pl.BlockSpec(memory_space=pltpu.SMEM)
ANY = pl.BlockSpec(memory_space=pl.ANY)
NN = (((1,), (0,)), ((), ()))
NT = (((1,), (1,)), ((), ()))
TN = (((0,), (0,)), ((), ()))


def dot(a, b, dims):
    return lax.dot_general(a, b, dims, precision=HIGHEST, preferred_element_type=F32)


def dot1(a, b, dims):
    return lax.dot_general(a, b, dims, preferred_element_type=F32)


def split(x):
    high = x.astype(BF16)
    return high, (x - high.astype(F32)).astype(BF16)


def split3(x):
    high = x.astype(BF16)
    rest = x - high.astype(F32)
    mid = rest.astype(BF16)
    return high, mid, (rest - mid.astype(F32)).astype(BF16)


def dot3(a, b, dims):
    ah, al = a
    bh, bl = b
    return dot1(ah, bh, dims) + (dot1(ah, bl, dims) + dot1(al, bh, dims))


def factor64(groups, f_ref):
    sub = lax.broadcasted_iota(jnp.int32, (8, 128), 0)

    def body(it, gs):
        cols = [[jnp.broadcast_to(g[:, t:t + 1], (8, 128)) for t in range(8)] for g in gs]
        rows = [jnp.broadcast_to(gs[0][t:t + 1, :], (8, 128)) for t in range(8)]
        s = [[jnp.broadcast_to(cols[0][t][u:u + 1, :], (8, 128)) if u >= t else None for t in range(8)] for u in range(8)]
        inv = [None] * 8
        for t in range(8):
            inv[t] = 1.0 / s[t][t]
            for u in range(t + 1, 8):
                low = s[u][t] * inv[t]
                for v in range(u, 8):
                    s[v][u] = s[v][u] - low * s[v][t]
                rows[u] = rows[u] - low * rows[t]
                for g in range(1, 8):
                    cols[g][u] = cols[g][u] - low * cols[g][t]
        done = jnp.zeros((8, 128), F32)
        for t in range(8):
            done = jnp.where(sub == t, rows[t] * lax.rsqrt(s[t][t]), done)
        f_ref[pl.ds(pl.multiple_of(it * 8, 8), 8), :] = pltpu.roll(done, it * 8, 1)
        scaled = [rows[t] * inv[t] for t in range(8)]
        left = []
        for g in range(1, 8):
            piece = gs[g]
            for t in range(8):
                piece = piece - cols[g][t] * scaled[t]
            left.append(pltpu.roll(piece, 120, 1))
        left.append(gs[0])
        return tuple(left)

    lax.fori_loop(0, 8, body, tuple(groups))


def factor256(x_ref, f_ref):
    lane = lax.broadcasted_iota(jnp.int32, (B, 128), 1)
    row = lax.broadcasted_iota(jnp.int32, (B, 128), 0)
    ident = (lane - B == row).astype(F32)
    col = lax.broadcasted_iota(jnp.int32, (B, T), 1)
    wide_row = lax.broadcasted_iota(jnp.int32, (B, T), 0)
    for k in range(T // B):
        lo = k * B
        strip = x_ref[lo:lo + B, :]
        block = strip[:, (k // 2) * 128:(k // 2) * 128 + 128]
        if k % 2:
            block = pltpu.roll(block, B, 1)
        both = jnp.where(lane < B, block, ident)
        factor64([both[8 * g:8 * g + 8, :] for g in range(8)], f_ref)
        block_inv = f_ref[...][:, B:]
        inside = (col >= lo) & (col < lo + B)
        strip = jnp.where(inside, (col - lo == wide_row).astype(F32), strip)
        out = dot(block_inv, strip, NN)
        x_ref[lo:lo + B, :] = jnp.where(col < lo + B, out, 0.0)
        if lo + B < T:
            rest = T - lo - B
            rest_col = lax.broadcasted_iota(jnp.int32, (rest, T), 1)
            old = x_ref[lo + B:, :]
            old = jnp.where((rest_col >= lo) & (rest_col < lo + B), 0.0, old)
            x_ref[lo + B:, :] = old - dot(out[:, lo + B:], out, TN)


def first_kernel(w00_ref, inv0_ref, f_ref):
    inv0_ref[...] = w00_ref[...]
    factor256(inv0_ref, f_ref)


def second_kernel(piv_ref, inv0_ref, w10_ref, w11_ref, l10_ref, inv1_ref, f_ref):
    l10 = dot(w10_ref[...], inv0_ref[...], NT)
    l10_ref[...] = l10
    inv1_ref[...] = jnp.zeros((T, T), F32)

    @pl.when(piv_ref[0] >= 2)
    def _():
        inv1_ref[...] = w11_ref[...] - dot(l10, l10, NT)
        factor256(inv1_ref, f_ref)


def panel_kernel(place_ref, slot_ref, inv0_ref, l10_ref, inv1_ref, front_ref, *refs):
    pieces = refs[:12]
    factor_ref, out_ref, yh_ref, yl_ref, tile_ref, sem = refs[12:]
    place = place_ref[0]
    a0 = split3(inv0_ref[...])
    low = split(l10_ref[...])
    inv1 = inv1_ref[...]
    for q in range(4):
        for r in range(2):
            if q == 0:
                p0 = front_ref[0, r, 0, :, 0:T]
                p1 = front_ref[0, r, 0, :, T:2 * T].astype(F32)
            else:
                p0 = pieces[(q - 1) * 4 + r * 2][...].astype(BF16)
                p1 = pieces[(q - 1) * 4 + r * 2 + 1][...]
            y0 = dot1(p0, a0[0], NT) + (dot1(p0, a0[1], NT) + dot1(p0, a0[2], NT))
            y0h, y0l = split(y0)
            p1 = p1 - dot3((y0h, y0l), low, NT)
            y1 = dot(p1, inv1, NT)
            if r == 0:
                owner = lax.rem(place + q, 4)
                y1 = jnp.where(owner > 0, y1, 0.0)
            y1h, y1l = split(y1)
            n = q * 2 + r
            yh_ref[n, :, 0:T] = y0h
            yl_ref[n, :, 0:T] = y0l
            yh_ref[n, :, T:2 * T] = y1h
            yl_ref[n, :, T:2 * T] = y1l
            if q == 0:
                factor_ref[0, r, 0, :, 0:T] = y0
                factor_ref[0, r, 0, :, T:2 * T] = y1
    copies = []
    for r in range(2):
        for n in range(8):
            column = lax.rem(place + n // 2, 4) + 4 * (n % 2)
            start = pl.multiple_of(column * T, T)
            tile = front_ref[0, r, 0, :, pl.ds(start, T)].astype(F32)
            own = (yh_ref[r], yl_ref[r])
            other = (yh_ref[n], yl_ref[n])
            tile_ref[r * 8 + n] = tile - dot3(own, other, NT)
            slot = slot_ref[r * 8 + column]
            copy = pltpu.make_async_copy(tile_ref.at[r * 8 + n], out_ref.at[jnp.maximum(slot, 0)], sem.at[r * 8 + n])

            @pl.when(slot >= 0)
            def _():
                copy.start()
            copies.append((slot, copy))
    for slot, copy in copies:
        @pl.when(slot >= 0)
        def _():
            copy.wait()


def add_kernel(target_ref, arrived_ref, out_ref):
    step = pl.program_id(0)

    @pl.when(step == 0)
    def _():
        out_ref[...] = jnp.zeros_like(out_ref)

    for i in range(4):
        target = target_ref[step * 4 + i]

        @pl.when(target >= 0)
        def _():
            out_ref[target] += arrived_ref[i]


def local(front, pivot_tiles, send_table):
    place = lax.axis_index("front").astype(jnp.int32)
    up = [(i, (i + 1) % 4) for i in range(4)]
    down = [(i, (i - 1) % 4) for i in range(4)]
    own = [[front[0, r, 0, :, k * T:k * T + T].astype(F32) for k in range(2)] for r in range(2)]
    from_left = [[None, None], [None, None]]
    from_right = [[None, None], [None, None]]
    from_far = [[None, None], [None, None]]
    for r in range(2):
        for k in range(2):
            from_left[r][k] = lax.ppermute(own[r][k], "front", up)
            from_right[r][k] = lax.ppermute(own[r][k], "front", down)
            if k == 0:
                from_far[r][k] = lax.ppermute(from_left[r][k], "front", up)
            else:
                from_far[r][k] = lax.ppermute(from_right[r][k], "front", down)
    by_q = [own, from_right, from_far, from_left]

    def of_owner(owner, r, k):
        q = lax.rem(owner - place + 4, 4)
        out = by_q[0][r][k]
        for i in range(1, 4):
            out = jnp.where(q == i, by_q[i][r][k], out)
        return out

    inv0 = pl.pallas_call(
        first_kernel,
        out_shape=jax.ShapeDtypeStruct((T, T), F32),
        in_specs=[VMEM],
        out_specs=VMEM,
        scratch_shapes=[pltpu.VMEM((B, 128), F32)],
        compiler_params=pltpu.CompilerParams(vmem_limit_bytes=16 << 20),
        name="first",
    )(of_owner(0, 0, 0))
    l10, inv1 = pl.pallas_call(
        second_kernel,
        out_shape=(jax.ShapeDtypeStruct((T, T), F32),) * 2,
        in_specs=[SMEM, VMEM, VMEM, VMEM],
        out_specs=(VMEM, VMEM),
        scratch_shapes=[pltpu.VMEM((B, 128), F32)],
        compiler_params=pltpu.CompilerParams(vmem_limit_bytes=16 << 20),
        name="second",
    )(pivot_tiles, inv0, of_owner(1, 0, 0), of_owner(1, 0, 1))

    table = send_table[0, 0]
    where = jnp.where(table[0] >= 0, table[0] * 8 + table[1], -1)
    ids = jnp.arange(64, dtype=jnp.int32)
    slots = jnp.max(jnp.where(where[None, :] == jnp.arange(16, dtype=jnp.int32)[:, None], ids[None, :], -1), axis=1)
    received = [by_q[q][r][k] for q in range(1, 4) for r in range(2) for k in range(2)]
    factor, outgoing = pl.pallas_call(
        panel_kernel,
        out_shape=(jax.ShapeDtypeStruct((1, 2, 1, T, 2 * T), F32), jax.ShapeDtypeStruct((64, T, T), F32)),
        in_specs=[SMEM, SMEM] + [VMEM] * 16,
        out_specs=(VMEM, ANY),
        scratch_shapes=[
            pltpu.VMEM((8, T, 2 * T), BF16),
            pltpu.VMEM((8, T, 2 * T), BF16),
            pltpu.VMEM((16, T, T), F32),
            pltpu.SemaphoreType.DMA((16,)),
        ],
        compiler_params=pltpu.CompilerParams(vmem_limit_bytes=40 << 20),
        name="panel",
    )(place.reshape(1), slots, inv0, l10, inv1, front, *received)
    arrived = lax.all_to_all(outgoing, "leaf", split_axis=0, concat_axis=0, tiled=True)
    targets = lax.all_to_all(table[2], "leaf", split_axis=0, concat_axis=0, tiled=True)
    ancestor = pl.pallas_call(
        add_kernel,
        out_shape=jax.ShapeDtypeStruct((ASLOT, T, T), F32),
        grid=(16,),
        in_specs=[SMEM, pl.BlockSpec((4, T, T), lambda i: (i, 0, 0))],
        out_specs=pl.BlockSpec((ASLOT, T, T), lambda i: (0, 0, 0)),
        compiler_params=pltpu.CompilerParams(vmem_limit_bytes=32 << 20),
        name="add",
    )(targets, arrived)
    return (factor, ancestor.reshape(1, 1, ASLOT, T, T))


def solution(mesh):
    in_specs = (P("leaf", None, "front", None, None), P("leaf"), P("leaf", "front", None, None))
    out_specs = (P("leaf", None, "front", None, None), P("leaf", "front", None, None, None))
    return jax.shard_map(local, mesh=mesh, in_specs=in_specs, out_specs=out_specs, check_vma=False)
```

time: 723 us -> 476 us (0.66); the launches traced: 714 us -> 475 us
  other arithmetic: 120 us -> 5.34 us
  local copies, waits for them, and re-layouts: 103 us -> 1.65 us
  waiting for transfers between devices: 426 us -> 376 us
  Pallas kernels: 0 us -> 36.6 us
  starting transfers between devices: 22.1 us -> 53.7 us
  matrix products: 24.3 us -> 0 us
  between operations: 18 us -> 1.44 us
    another operation x18 -> x0, other arithmetic: 109 us -> none  [the longest x13 68.7 us: solve_panel(): factor_tile = jnp.linalg.cholesky(diagonal)]
    all_gather x2 -> x0, waiting for transfers between devices: 57 us -> none  [local(): lax.all_gather(piece, 'front', axis=1, tiled=True).reshape(width, tile)]
    pallas_call x0 -> x4, Pallas kernels: none -> 36.6 us  [the longest x1 13.4 us: local(): pl.pallas_call(add_kernel, out_shape=jax.ShapeDtypeStruct((ASLOT, T, T),...]
    unnamed x11 -> x8, local copies, waits for them, and re-layouts: 27.9 us -> 0.96 us
    select_n x1 -> x0, local copies, waits for them, and re-layouts: 20.2 us -> none  [local(): jnp.where(live[:, None], jnp.take(tiles_all, position, axis=0), 0.0)]
    gather x1 -> x0, local copies, waits for them, and re-layouts: 20.2 us -> none  [local(): jnp.take(tiles_all, position, axis=0)]
    dot_general x3 -> x0, matrix products: 16.9 us -> none  [the longest x2 11.3 us: local(): work = work - jnp.dot(mine, solved.T, precision=highest)]
    ppermute x0 -> x12, starting transfers between devices: none -> 15.5 us  [the longest x4 8.69 us: local(): from_right[r][k] = lax.ppermute(own[r][k], 'front', down)]
  transfers between devices with their start and end apart: 4 -> 14, of which waited for: 3 -> 3; matrix products, arithmetic and copies ran while one was open for 19% -> 1% of each run, Pallas kernels for 0% -> 5%
where the time goes in v1:
time: 476 us; the launch traced here: 475 us
  waiting for transfers between devices  376 us (79%)
  starting transfers between devices  53.7 us (11%)
  Pallas kernels  36.6 us (8%)
  other arithmetic  5.34 us (1%)
    all_to_all x1, waiting for transfers between devices, local(): lax.all_to_all(outgoing, 'leaf', split_axis=0, concat_axis=0, tiled=True)  371 us
    all_to_all x1, starting transfers between devices, local(): lax.all_to_all(outgoing, 'leaf', split_axis=0, concat_axis=0, tiled=True)  24 us
    all_to_all x1, starting transfers between devices, local(): lax.all_to_all(table[2], 'leaf', split_axis=0, concat_axis=0, tiled=True)  14.2 us
    pallas_call x1, Pallas kernels, local(): pl.pallas_call(add_kernel, out_shape=jax.ShapeDtypeStruct((ASLOT, T, T),...  13.4 us
    pallas_call x1, Pallas kernels, local(): pl.pallas_call(first_kernel, out_shape=jax.ShapeDtypeStruct((T, T), F32),...  12.1 us
    pallas_call x1, Pallas kernels, local(): pl.pallas_call(panel_kernel, out_shape=(jax.ShapeDtypeStruct((1, 2, 1, T,...  10.7 us
  transfers between devices with their start and end apart: 14, of which 3 were waited for; matrix products, arithmetic and copies ran while one was open for 1% of the time, Pallas kernels for 5%

profile of v1, /device:TPU:49, one launch (start us, length us, event | category | flops | bytes accessed | tf_op | source)
XLA Modules:
  0.0 475.1 jit_solution(18155271336491496532)
XLA Ops:
  0.6 0.0 copy-start
  0.6 2.1 bitcast_convert_fusion
  2.8 0.0 copy-start.3
  2.8 2.5 collective-permute-start.7
  5.3 0.5 collective-permute-start.4
  5.8 0.9 collective-permute-start
  6.7 0.0 collective-permute-start.3
  6.8 2.6 collective-permute-start.2
  9.4 0.8 collective-permute-done.7.refs_3_
  10.2 0.0 copy-start.1
  10.2 1.0 collective-permute-start.8
  11.2 0.0 copy-done.1
  11.2 4.8 %collective-permute-done.4.refs_1_ = f32[256,256]{1,0:T(8,128)S(1)} collective-permute-done((f32[256,256]{1,0:T(8,128)}, f32[256,256]{1,0:T(8,128)S(1)}, u32[]{:S(2)}, u32[]{:S(2)}) %collective-permute-start.4) | collective-permute-done | bytes 262176 | tf_op jit(solution)/shard_map/ppermute | solution.py:207
  15.9 3.3 collective-permute-start.5
  19.2 0.0 collective-permute-done.refs_8_
  19.2 0.0 copy-done.3
  19.2 0.0 collective-permute-start.1
  19.2 0.7 slice_bitcast_fusion
  19.9 0.7 copy.7
  20.6 14.2 %all-to-all-start = ((s32[64,1,1]{2,1,0:T(1,128)}), s32[64,1,1]{2,1,0:T(1,128)S(1)}, u32[]{:S(2)}, u32[]{:S(2)}) async-start(s32[64,1,1]{2,1,0:T(1,128)} %copy.7), calls=%async_computation | async-start | bytes 65536 | tf_op jit(solution)/shard_map/all_to_all | solution.py:260
  35.5 0.1 select_reduce_fusion.slot_ref
  35.6 0.0 collective-permute-done.8.refs_10_
  35.6 0.1 collective-permute-start.11
  35.7 0.0 collective-permute-done.3.refs_9_
  35.7 3.0 collective-permute-start.6
  38.8 0.0 collective-permute-done.2.refs_0_
  38.8 1.4 collective-permute-start.10
  40.1 0.0 collective-permute-done.5.refs_5_
  40.1 0.1 collective-permute-start.9
  40.2 0.0 collective-permute-done.1.refs_4_
  40.2 1.2 select_select_fusion.1
  41.4 12.1 %first.1.inv0_ref = f32[256,256]{1,0:T(8,128)S(1)} custom-call(f32[256,256]{1,0:T(8,128)S(1)} %get-tuple-element.11.w00_ref), custom_call_target="tpu_custom_call" | custom-call | tf_op jit(solution)/shard_map/first/pallas_call | solution.py:221
  53.5 0.4 second.1
  53.9 0.0 collective-permute-done.11.refs_11_
  53.9 0.0 collective-permute-done.6.refs_2_
  53.9 0.0 collective-permute-done.10.refs_7_
  54.0 0.0 collective-permute-done.9.refs_6_
  54.0 0.0 copy-done
  54.0 0.0 copy-start.2
  54.0 0.9 copy-done.2
  54.9 10.7 %panel.1 = (f32[1,2,1,256,512]{4,3,2,1,0:T(8,128)}, f32[64,256,256]{2,1,0:T(8,128)}) custom-call(s32[1]{0:T(128)} %bitcast.place_ref, s32[16]{0:T(128)S(1)} %select_reduce_fusion.slot_ref, f32[256,256]{1,0:T(8,128)S(1)} %first.1.inv0_ref, f32[256,256]{1,0:T(8,128)S(1)} %get-tuple-element.6.l10_ref, f32[256,256]{1,0:T(8,128)S(1)} %get-tuple-element.7.inv1_ref, ...), custom_call_target="tpu_custom_call" | custom-call | tf_op jit(solution)/shard_map/panel/pallas_call | solution.py:245
  65.6 0.0 all-to-all-done
  65.6 24.0 %all-to-all-start.1 = ((f32[64,256,256]{2,1,0:T(8,128)}), f32[64,256,256]{2,1,0:T(8,128)}, u32[]{:S(2)}, u32[]{:S(2)}) async-start(f32[64,256,256]{2,1,0:T(8,128)} %get-tuple-element.9), calls=%async_computation.1 | async-start | bytes 33554432 | tf_op jit(solution)/shard_map/all_to_all | solution.py:259
  89.6 1.2 reduce.target_ref
  90.9 370.8 %all-to-all-done.1.arrived_ref = f32[64,256,256]{2,1,0:T(8,128)} async-done(((f32[64,256,256]{2,1,0:T(8,128)}), f32[64,256,256]{2,1,0:T(8,128)}, u32[]{:S(2)}, u32[]{:S(2)}) %all-to-all-start.1) | async-done | bytes 16777248 | tf_op jit(solution)/shard_map/all_to_all | solution.py:259
  461.6 13.4 %add.23 = f32[16,256,256]{2,1,0:T(8,128)} custom-call(s32[64]{0:T(128)S(1)} %reduce.target_ref, f32[64,256,256]{2,1,0:T(8,128)} %all-to-all-done.1.arrived_ref), custom_call_target="tpu_custom_call" | custom-call | tf_op jit(solution)/shard_map/add/pallas_call | solution.py:261
Async XLA Ops:
  0.6 53.3 %copy-start = (bf16[1,2,1,256,2048]{4,3,2,1,0:T(8,128)(2,1)S(1)}, bf16[1,2,1,256,2048]{4,3,2,1,0:T(8,128)(2,1)}, u32[]{:S(2)}) copy-start(bf16[1,2,1,256,2048]{4,3,2,1,0:T(8,128)(2,1)} %front_ref.1) | copy-start | bytes 6291460
  2.8 16.5 %copy-start.3 = (f32[256,256]{1,0:T(8,128)}, f32[256,256]{1,0:T(8,128)S(1)}, u32[]{:S(2)}) copy-start(f32[256,256]{1,0:T(8,128)S(1)} %get-tuple-element.12) | copy-start | bytes 786436
  2.8 7.4 %collective-permute-start.7 = (f32[256,256]{1,0:T(8,128)S(1)}, f32[256,256]{1,0:T(8,128)S(1)}, u32[]{:S(2)}, u32[]{:S(2)}) collective-permute-start(f32[256,256]{1,0:T(8,128)S(1)} %get-tuple-element.12), channel_id=1, source_target_pairs={{0,3},{1,0},{2,1},{3,2},{4,7},{5,4},{6,5},{7,6},{8,11},{9,8},{10,9... | collective-permute-start | bytes 786440 | tf_op jit(solution)/shard_map/ppermute | solution.py:207
  5.3 10.7 %collective-permute-start.4 = (f32[256,256]{1,0:T(8,128)}, f32[256,256]{1,0:T(8,128)S(1)}, u32[]{:S(2)}, u32[]{:S(2)}) collective-permute-start(f32[256,256]{1,0:T(8,128)} %get-tuple-element.14), channel_id=1, source_target_pairs={{0,3},{1,0},{2,1},{3,2},{4,7},{5,4},{6,5},{7,6},{8,11},{9,8},{10,9... | collective-permute-start | bytes 786440 | tf_op jit(solution)/shard_map/ppermute | solution.py:207
  5.8 13.4 %collective-permute-start = (f32[256,256]{1,0:T(8,128)}, f32[256,256]{1,0:T(8,128)S(1)}, u32[]{:S(2)}, u32[]{:S(2)}) collective-permute-start(f32[256,256]{1,0:T(8,128)} %get-tuple-element.15), channel_id=1, source_target_pairs={{0,1},{1,2},{2,3},{3,0},{4,5},{5,6},{6,7},{7,4},{8,9},{9,10},{10,1... | collective-permute-start | bytes 786440 | tf_op jit(solution)/shard_map/ppermute | solution.py:206
  6.7 29.0 %collective-permute-start.3 = (f32[256,256]{1,0:T(8,128)}, f32[256,256]{1,0:T(8,128)S(1)}, u32[]{:S(2)}, u32[]{:S(2)}) collective-permute-start(f32[256,256]{1,0:T(8,128)} %get-tuple-element.14), channel_id=1, source_target_pairs={{0,1},{1,2},{2,3},{3,0},{4,5},{5,6},{6,7},{7,4},{8,9},{9,10},{10,1... | collective-permute-start | bytes 786440 | tf_op jit(solution)/shard_map/ppermute | solution.py:206
  6.8 32.0 %collective-permute-start.2 = (f32[256,256]{1,0:T(8,128)}, f32[256,256]{1,0:T(8,128)S(1)}, u32[]{:S(2)}, u32[]{:S(2)}) collective-permute-start(f32[256,256]{1,0:T(8,128)} %get-tuple-element.15), channel_id=1, source_target_pairs={{0,3},{1,0},{2,1},{3,2},{4,7},{5,4},{6,5},{7,6},{8,11},{9,8},{10,9... | collective-permute-start | bytes 786440 | tf_op jit(solution)/shard_map/ppermute | solution.py:207
  10.2 1.0 copy-start.1
  10.2 25.4 %collective-permute-start.8 = (f32[256,256]{1,0:T(8,128)}, f32[256,256]{1,0:T(8,128)}, u32[]{:S(2)}, u32[]{:S(2)}) collective-permute-start(f32[256,256]{1,0:T(8,128)} %get-tuple-element.13), channel_id=1, source_target_pairs={{0,1},{1,2},{2,3},{3,0},{4,5},{5,6},{6,7},{7,4},{8,9},{9,10},{10,1... | collective-permute-start | bytes 786440 | tf_op jit(solution)/shard_map/ppermute | solution.py:206
  15.9 24.2 %collective-permute-start.5 = (f32[256,256]{1,0:T(8,128)S(1)}, f32[256,256]{1,0:T(8,128)S(1)}, u32[]{:S(2)}, u32[]{:S(2)}) collective-permute-start(f32[256,256]{1,0:T(8,128)S(1)} %collective-permute-done.4.refs_1_), channel_id=1, source_target_pairs={{0,3},{1,0},{2,1},{3,2},{4,7},{5,4},{6,5},{7,6},{8,11},{9,8},{10,9... | collective-permute-start | bytes 786440 | tf_op jit(solution)/shard_map/ppermute | solution.py:211
  19.2 21.0 %collective-permute-start.1 = (f32[256,256]{1,0:T(8,128)S(1)}, f32[256,256]{1,0:T(8,128)}, u32[]{:S(2)}, u32[]{:S(2)}) collective-permute-start(f32[256,256]{1,0:T(8,128)S(1)} %collective-permute-done.refs_8_), channel_id=1, source_target_pairs={{0,1},{1,2},{2,3},{3,0},{4,5},{5,6},{6,7},{7,4},{8,9},{9,10},{10,1... | collective-permute-start | bytes 786440 | tf_op jit(solution)/shard_map/ppermute | solution.py:209
  20.6 45.0 %all-to-all-start = ((s32[64,1,1]{2,1,0:T(1,128)}), s32[64,1,1]{2,1,0:T(1,128)S(1)}, u32[]{:S(2)}, u32[]{:S(2)}) async-start(s32[64,1,1]{2,1,0:T(1,128)} %copy.7), calls=%async_computation | async-start | bytes 65536 | tf_op jit(solution)/shard_map/all_to_all | solution.py:260
  35.6 18.3 %collective-permute-start.11 = (f32[256,256]{1,0:T(8,128)}, f32[256,256]{1,0:T(8,128)S(1)}, u32[]{:S(2)}, u32[]{:S(2)}) collective-permute-start(f32[256,256]{1,0:T(8,128)} %copy-done.3), channel_id=1, source_target_pairs={{0,1},{1,2},{2,3},{3,0},{4,5},{5,6},{6,7},{7,4},{8,9},{9,10},{10,1... | collective-permute-start | bytes 786440 | tf_op jit(solution)/shard_map/ppermute | solution.py:206
  35.7 18.2 %collective-permute-start.6 = (f32[256,256]{1,0:T(8,128)}, f32[256,256]{1,0:T(8,128)S(1)}, u32[]{:S(2)}, u32[]{:S(2)}) collective-permute-start(f32[256,256]{1,0:T(8,128)} %get-tuple-element.13), channel_id=1, source_target_pairs={{0,3},{1,0},{2,1},{3,2},{4,7},{5,4},{6,5},{7,6},{8,11},{9,8},{10,9... | collective-permute-start | bytes 786440 | tf_op jit(solution)/shard_map/ppermute | solution.py:207
  38.8 15.2 %collective-permute-start.10 = (f32[256,256]{1,0:T(8,128)}, f32[256,256]{1,0:T(8,128)S(1)}, u32[]{:S(2)}, u32[]{:S(2)}) collective-permute-start(f32[256,256]{1,0:T(8,128)} %copy-done.1), channel_id=1, source_target_pairs={{0,3},{1,0},{2,1},{3,2},{4,7},{5,4},{6,5},{7,6},{8,11},{9,8},{10,9... | collective-permute-start | bytes 786440 | tf_op jit(solution)/shard_map/ppermute | solution.py:211
  40.1 13.8 %collective-permute-start.9 = (f32[256,256]{1,0:T(8,128)}, f32[256,256]{1,0:T(8,128)S(1)}, u32[]{:S(2)}, u32[]{:S(2)}) collective-permute-start(f32[256,256]{1,0:T(8,128)} %collective-permute-done.8.refs_10_), channel_id=1, source_target_pairs={{0,1},{1,2},{2,3},{3,0},{4,5},{5,6},{6,7},{7,4},{8,9},{9,10},{10,1... | collective-permute-start | bytes 786440 | tf_op jit(solution)/shard_map/ppermute | solution.py:209
  54.0 1.0 copy-start.2
  65.6 396.0 %all-to-all-start.1 = ((f32[64,256,256]{2,1,0:T(8,128)}), f32[64,256,256]{2,1,0:T(8,128)}, u32[]{:S(2)}, u32[]{:S(2)}) async-start(f32[64,256,256]{2,1,0:T(8,128)} %get-tuple-element.9), calls=%async_computation.1 | async-start | bytes 33554432 | tf_op jit(solution)/shard_map/all_to_all | solution.py:259

commit v2 on v1

--- a/solution.py
+++ b/solution.py
@@ -9,6 +9,16 @@
 
 PT = 2
 ASLOT = 16
+TILES = 14
+N1, N2 = 15, 10
+FY1, FY2 = 9, 6
+FZ3, FZ4 = 10, 7
+NY1, NY2 = 18, 12
+BUF, ZN1, ZN2, YF1, YF2, YN1, YN2, ZF3, ZF4, ROOT = range(10)
+N_CUT = (0, 5, 10, 15)
+FY_CUT = (0, 6, 9)
+FZ_CUT = (0, 4, 7, 10)
+NY_CUT = (0, 6, 12, 18)
 B = 64
 T = 256
 F32 = jnp.float32
@@ -125,9 +135,107 @@
         factor256(inv1_ref, f_ref)
 
 
-def panel_kernel(place_ref, slot_ref, inv0_ref, l10_ref, inv1_ref, front_ref, *refs):
+def iota(shape, dim):
+    return lax.broadcasted_iota(jnp.int32, shape, dim)
+
+
+def fdot(a, b):
+    return lax.dot_general(a, b, (((1,), (0,)), ((), ())), preferred_element_type=F32)
+
+
+def route(codes, z, y, c):
+    shape, sq, rows = (32, 128), (128, 128), (32, 32)
+    row, lane = iota(shape, 0), iota(shape, 1)
+    zs, ys = row // 4, row % 4
+    cs, zd, yd, cd = lane // 64, (lane // 8) % 8, (lane // 2) % 4, lane % 2
+    dz, dy = (zd - zs + 8) % 8, (yd - ys + 4) % 4
+    hops = jnp.minimum(dz, 8 - dz)
+    far = hops > 2
+    live = (codes >= 0) & ~((lane % 64 == 0) & far)
+    tile = jnp.where(live, codes // 16, 0)
+    slot = jnp.where(live, codes % 16, 0)
+    la, lb = iota(sq, 0), iota(sq, 1)
+    before = la < lb
+    same_zd = (la // 8) % 8 == (lb // 8) % 8
+    same_yd = (la // 2) % 4 == (lb // 2) % 4
+    ra, rb = iota(rows, 0), iota(rows, 1)
+    same_ys = ra % 4 == rb % 4
+    same_zs = ra // 4 == rb // 4
+
+    def f(x):
+        return x.astype(F32)
+
+    def count(mask, lanes, peers):
+        rank = fdot(f(mask), f(before & lanes))
+        total = fdot(f(mask), f(lanes))
+        if peers is not None:
+            rank = rank + fdot(f(peers & (rb < ra)), total)
+            total = fdot(f(peers), total)
+        return rank, total
+
+    def halves(n_up, n_both, n_down):
+        up = jnp.clip(jnp.floor((n_both + n_down - n_up + 1.0) * 0.5), 0.0, n_both)
+        return up, n_both - up
+
+    every = la >= 0
+    over = jnp.full(shape, -1.0, F32)
+    r1, n1 = count(live & (dz == 1), every, None)
+    r2, n2 = count(live & (dz == 2), every, None)
+    r6, n6 = count(live & (dz == 6), every, None)
+    r7, n7 = count(live & (dz == 7), every, None)
+    zpos = jnp.where(dz == 1, n2 + r1, jnp.where(dz == 2, r2, jnp.where(dz == 6, r6, n6 + r7)))
+    over = jnp.maximum(over, jnp.maximum(n1 + n2, n7 + n6) - N1)
+    over = jnp.maximum(over, jnp.maximum(n2, n6) - N2)
+
+    def ring(mask, lanes, peers, near, distant):
+        a1, m1 = count(mask & (dy == 1), lanes, peers)
+        a2, m2 = count(mask & (dy == 2), lanes, peers)
+        a3, m3 = count(mask & (dy == 3), lanes, peers)
+        up, down = halves(m1, m2, m3)
+        minus = (dy == 3) | ((dy == 2) & (a2 >= up))
+        pos = jnp.where(dy == 1, up + a1, jnp.where(dy == 3, down + a3, jnp.where(a2 < up, a2, a2 - up)))
+        excess = jnp.maximum(jnp.maximum(up + m1, down + m3) - near, jnp.maximum(up, down) - distant)
+        return minus.astype(jnp.int32), pos.astype(jnp.int32), excess
+
+    fy_core, fy_pos, excess = ring(live & far, every, None, FY1, FY2)
+    over = jnp.maximum(over, excess)
+    r3, n3 = count(live & (dz == 3), same_yd, same_zs)
+    r4, n4 = count(live & (dz == 4), same_yd, same_zs)
+    r5, n5 = count(live & (dz == 5), same_yd, same_zs)
+    up, down = halves(n3, n4, n5)
+    fz_pos = jnp.where(dz == 3, up + r3, jnp.where(dz == 5, down + r5, jnp.where(r4 < up, r4, r4 - up)))
+    over = jnp.maximum(over, jnp.maximum(up + n3, down + n5) - FZ3)
+    over = jnp.maximum(over, jnp.maximum(up, down) - FZ4)
+    z_core = ((dz > 4) | ((dz == 4) & (r4 >= up))).astype(jnp.int32)
+    ny_core, ny_pos, excess = ring(live & ~far, same_zd, same_ys, NY1, NY2)
+    over = jnp.maximum(over, excess)
+    zpos, fz_pos = zpos.astype(jnp.int32), fz_pos.astype(jnp.int32)
+
+    def source(kind, core, held):
+        return (kind * 2 + (core != c)) * 32 + held
+
+    here = live & (row == z * 4 + y)
+    queued = jnp.sum(jnp.where(here & ~far & (dz > 0) & (z_core == c), source(BUF, cs, tile) * 32 + zpos + 1, 0), axis=0, keepdims=True) - 1
+    queued_far = jnp.sum(jnp.where(here & far & (dy > 0) & (fy_core == c), source(BUF, cs, tile) * 32 + fy_pos + 1, 0), axis=0, keepdims=True) - 1
+    after_y = jnp.where(dy == 0, source(BUF, cs, tile), source(jnp.where(dy == 2, YF2, YF1), fy_core, fy_pos))
+    turn_far = jnp.where(live & far & (zs == z) & (yd == y) & (z_core == c), after_y * 32 + fz_pos, -1)
+    after_z = jnp.where(dz == 0, source(BUF, cs, tile), source(jnp.where(hops == 1, ZN1, ZN2), z_core, zpos))
+    turn_near = jnp.where(live & ~far & (zd == z) & (ys == y) & (dy > 0) & (ny_core == c), after_z * 32 + ny_pos, -1)
+    end_near = jnp.where(dy == 0, after_z, source(jnp.where(dy == 2, YN2, YN1), ny_core, ny_pos))
+    end_far = source(jnp.where(dz == 4, ZF4, ZF3), z_core, fz_pos)
+    mine = live & (zd == z) & (yd == y) & (cd == c)
+    end = jnp.where(mine, jnp.where(far, end_far, end_near) * 16 + slot, -1)
+    return queued, queued_far, turn_near, turn_far, end, jnp.max(over, keepdims=True)
+
+
+def plan_kernel(where_ref, codes_ref, *out_refs):
+    for ref, value in zip(out_refs, route(codes_ref[...], where_ref[0], where_ref[1], where_ref[2])):
+        ref[...] = value
+
+
+def panel_kernel(place_ref, first_ref, inv0_ref, l10_ref, inv1_ref, front_ref, *refs):
     pieces = refs[:12]
-    factor_ref, out_ref, yh_ref, yl_ref, tile_ref, sem = refs[12:]
+    factor_ref, out_ref, zero_ref, yh_ref, yl_ref = refs[12:]
     place = place_ref[0]
     a0 = split3(inv0_ref[...])
     low = split(l10_ref[...])
@@ -156,26 +264,175 @@
             if q == 0:
                 factor_ref[0, r, 0, :, 0:T] = y0
                 factor_ref[0, r, 0, :, T:2 * T] = y1
-    copies = []
     for r in range(2):
         for n in range(8):
             column = lax.rem(place + n // 2, 4) + 4 * (n % 2)
-            start = pl.multiple_of(column * T, T)
-            tile = front_ref[0, r, 0, :, pl.ds(start, T)].astype(F32)
-            own = (yh_ref[r], yl_ref[r])
-            other = (yh_ref[n], yl_ref[n])
-            tile_ref[r * 8 + n] = tile - dot3(own, other, NT)
-            slot = slot_ref[r * 8 + column]
-            copy = pltpu.make_async_copy(tile_ref.at[r * 8 + n], out_ref.at[jnp.maximum(slot, 0)], sem.at[r * 8 + n])
-
-            @pl.when(slot >= 0)
+
+            @pl.when(column > 0)
             def _():
-                copy.start()
-            copies.append((slot, copy))
-    for slot, copy in copies:
-        @pl.when(slot >= 0)
+                start = pl.multiple_of(column * T, T)
+                tile = front_ref[0, r, 0, :, pl.ds(start, T)].astype(F32)
+                own = (yh_ref[r], yl_ref[r])
+                other = (yh_ref[n], yl_ref[n])
+                tile = tile - dot3(own, other, NT)
+                index = r * 7 + column - 1
+                out_ref[index] = tile
+
+                @pl.when(index == first_ref[0])
+                def _():
+                    zero_ref[...] = tile
+
+
+def pieces_of(kind, cut, own, sib=None):
+    spans = [(kind * 2, lo, hi, x) for lo, hi, x in zip(cut, cut[1:], own)]
+    if sib is not None:
+        spans += [(kind * 2 + 1, lo, hi, x) for lo, hi, x in zip(cut, cut[1:], sib)]
+    return spans
+
+
+def copy_from(sources, source, held, target_ref, sem):
+    for sid, lo, hi, ref in sources:
+        @pl.when((source == sid) & (held >= lo) & (held < hi))
         def _():
-            copy.wait()
+            pltpu.make_async_copy(ref.at[held - lo], target_ref, sem).start()
+
+
+def gather_kernel(spans, cut, entries, where_ref, table_ref, *refs):
+    sources = [span + (ref,) for span, ref in zip(spans, refs)]
+    outs = refs[len(spans):-1]
+    sem = refs[-1]
+
+    def each(act):
+        def body(e, _):
+            code = table_ref[entries(e, where_ref[0], where_ref[1], where_ref[2])]
+
+            @pl.when(code >= 0)
+            def _():
+                act(code // 1024, (code // 32) % 32, code % 32)
+            return 0
+
+        lax.fori_loop(0, 128, body, 0)
+
+    def start(source, held, pos):
+        for lo, hi, out in zip(cut, cut[1:], outs):
+            @pl.when((pos >= lo) & (pos < hi))
+            def _():
+                copy_from(sources, source, held, out.at[pos - lo], sem.at[pos])
+
+    def wait(source, held, pos):
+        pltpu.make_async_copy(refs[0].at[0], outs[0].at[0], sem.at[pos]).wait()
+
+    each(start)
+    each(wait)
+
+
+def chip_entries(e, z, y, c):
+    return 0, e
+
+
+def near_entries(e, z, y, c):
+    return (e // 16) * 4 + y, ((e // 8) % 2) * 64 + z * 8 + e % 8
+
+
+def far_entries(e, z, y, c):
+    return z * 4 + e // 32, (e // 2 % 16) * 8 + y * 2 + e % 2
+
+
+def gather(where, table, spans, cut, entries, name):
+    return pl.pallas_call(
+        lambda *refs: gather_kernel([span[:3] for span in spans], cut, entries, *refs),
+        out_shape=tiles(*[hi - lo for lo, hi in zip(cut, cut[1:])]),
+        in_specs=[SMEM, SMEM] + [ANY] * len(spans),
+        out_specs=(VMEM,) * (len(cut) - 1),
+        scratch_shapes=[pltpu.SemaphoreType.DMA((cut[-1],))],
+        compiler_params=pltpu.CompilerParams(vmem_limit_bytes=16 << 20),
+        name=name,
+    )(where, table, *[span[3] for span in spans])
+
+
+DEPTH = 8
+
+
+def sum_kernel(spans, first, last, where_ref, table_ref, codes_ref, base_ref, *refs):
+    z, y, c = where_ref[0], where_ref[1], where_ref[2]
+    sources = [span + (ref,) for span, ref in zip(spans, refs)]
+    out_ref, list_ref, buf_ref, sem = refs[len(spans):]
+    if first == BUF:
+        out_ref[...] = jnp.zeros_like(out_ref)
+    else:
+        out_ref[...] = base_ref[...]
+
+    def collect(i, n):
+        code = table_ref[i // 2, (i % 2) * 64 + z * 8 + y * 2 + c]
+        kind = code // 1024
+        take = (code >= 0) & (kind >= first) & (kind <= last)
+
+        @pl.when(take)
+        def _():
+            list_ref[n] = code
+        return n + take.astype(jnp.int32)
+
+    n = lax.fori_loop(0, 64, collect, jnp.int32(0))
+    if first == BUF:
+        def collect_root(i, n):
+            code = codes_ref[12 + i // 2, (i % 2) * 64]
+            list_ref[n] = ((ROOT + (i // 2) % 4) * 64 + (i // 8) * 2 + i % 2) * 16 + code % 16
+            return n + 1
+
+        n = lax.fori_loop(0, jnp.where((z == 0) & (y == 0) & (c == 0), 24, 0), collect_root, n)
+
+    def start(i):
+        code = list_ref[i]
+        slot = lax.rem(i, DEPTH)
+        copy_from(sources, code // 512, (code // 16) % 32, buf_ref.at[slot], sem.at[slot])
+
+    def prime(i, _):
+        start(i)
+        return 0
+
+    def step(i, _):
+        slot = lax.rem(i, DEPTH)
+        pltpu.make_async_copy(refs[0].at[0], buf_ref.at[slot], sem.at[slot]).wait()
+        out_ref[list_ref[i] % 16] += buf_ref[slot]
+
+        @pl.when(i + DEPTH < n)
+        def _():
+            start(i + DEPTH)
+        return 0
+
+    lax.fori_loop(0, jnp.minimum(n, DEPTH), prime, 0)
+    lax.fori_loop(0, n, step, 0)
+
+
+def add_up(where, table, codes, base, spans, first, last, name):
+    return pl.pallas_call(
+        lambda *refs: sum_kernel([span[:3] for span in spans], first, last, *refs),
+        out_shape=tiles(ASLOT)[0],
+        in_specs=[SMEM, SMEM, SMEM, VMEM] + [ANY] * len(spans),
+        out_specs=VMEM,
+        scratch_shapes=[pltpu.SMEM((256,), jnp.int32), pltpu.VMEM((DEPTH, T, T), F32), pltpu.SemaphoreType.DMA((DEPTH,))],
+        compiler_params=pltpu.CompilerParams(vmem_limit_bytes=32 << 20),
+        name=name,
+    )(where, table, codes, base, *[span[3] for span in spans])
+
+
+def slots_kernel(tile_ref, own_ref, out_ref, sem):
+    def start(p, _):
+        tile = tile_ref[p]
+
+        @pl.when(tile >= 0)
+        def _():
+            pltpu.make_async_copy(own_ref.at[tile], out_ref.at[p], sem.at[p]).start()
+        return 0
+
+    def wait(p, _):
+        @pl.when(tile_ref[p] >= 0)
+        def _():
+            pltpu.make_async_copy(own_ref.at[0], out_ref.at[p], sem.at[p]).wait()
+        return 0
+
+    lax.fori_loop(0, 64, start, 0)
+    lax.fori_loop(0, 64, wait, 0)
 
 
 def add_kernel(target_ref, arrived_ref, out_ref):
@@ -193,26 +450,133 @@
             out_ref[target] += arrived_ref[i]
 
 
+def tiles(*counts):
+    return tuple(jax.ShapeDtypeStruct((n, T, T), F32) for n in counts)
+
+
+def leaf_id(z, y, c):
+    return ((z % 8) * 4 + y % 4) * 2 + c
+
+
+PLACES = [(z, y, c) for z in range(8) for y in range(4) for c in range(2)]
+
+
+def send(x, pairs):
+    return lax.ppermute(x, "leaf", [(leaf_id(*a), leaf_id(*b)) for a, b in pairs])
+
+
+def dense(work, zero, tile, slot, codes, where, *tables):
+    outgoing = pl.pallas_call(
+        slots_kernel,
+        out_shape=tiles(64)[0],
+        in_specs=[SMEM, ANY],
+        out_specs=ANY,
+        scratch_shapes=[pltpu.SemaphoreType.DMA((64,))],
+        name="slots",
+    )(tile, work)
+    arrived = lax.all_to_all(outgoing, "leaf", split_axis=0, concat_axis=0, tiled=True)
+    targets = lax.all_to_all(slot, "leaf", split_axis=0, concat_axis=0, tiled=True)
+    return pl.pallas_call(
+        add_kernel,
+        out_shape=tiles(ASLOT)[0],
+        grid=(16,),
+        in_specs=[SMEM, pl.BlockSpec((4, T, T), lambda i: (i, 0, 0))],
+        out_specs=pl.BlockSpec((ASLOT, T, T), lambda i: (0, 0, 0)),
+        compiler_params=pltpu.CompilerParams(vmem_limit_bytes=32 << 20),
+        name="add",
+    )(targets, arrived)
+
+
+def tie(x, *others):
+    return lax.optimization_barrier((x,) + others)[0]
+
+
+def sparse(work, zero, tile, slot, codes, where, queued, queued_far, turn_near, turn_far, end):
+    swap = [((z, y, c), (z, y, 1 - c)) for z, y, c in PLACES]
+    along_z = [((z, y, c), (z + 1 - 2 * c, y, c)) for z, y, c in PLACES]
+    along_y = [((z, y, c), (z, y + 1 - 2 * c, c)) for z, y, c in PLACES]
+
+    def sends(xs, pairs):
+        return [send(x, pairs) for x in xs]
+
+    def after(xs, *others):
+        n = len(xs)
+        return list(lax.optimization_barrier(tuple(xs) + others)[:n])
+
+    other = send(work, swap)
+    root = [send(zero, [((z, y, c), (0, y, 0)) for y in range(4)]) for z in (3, 4, 5) for c in range(2)]
+    both = pieces_of(BUF, (0, TILES), [work], [other])
+    far_out = gather(where, queued_far, both, FY_CUT, chip_entries, "queue_far")
+    near_out = gather(where, queued, both, N_CUT, chip_entries, "queue")
+    near_out, far_out = after(near_out, *far_out), after(far_out, *near_out)
+    n1 = sends(near_out, along_z)
+    f1 = sends(far_out, along_y)
+    f2 = sends(after(f1[:1], f1[1]), along_y)
+    n2 = sends(after(n1[:2], n1[2], *f1), along_z)
+    f1_other, f2_other, n1_other = sends(f1, swap), sends(f2, swap), sends(n1, swap)
+    lists = gather(
+        where, turn_far,
+        both + pieces_of(YF1, FY_CUT, f1, f1_other) + pieces_of(YF2, FY_CUT[:2], f2, f2_other),
+        FZ_CUT, far_entries, "turn_far")
+    z1 = sends(after(lists, *n2), along_z)
+    n2_other = sends(n2, swap)
+    near_spans = both + pieces_of(ZN1, N_CUT, n1, n1_other) + pieces_of(ZN2, N_CUT[:3], n2, n2_other)
+    lists = gather(where, turn_near, near_spans, NY_CUT, near_entries, "turn_near")
+    column = jnp.stack(after(root, *n2))
+    pass_on = send(column, [((0, 2, 0), (0, 1, 0))])
+    row1 = send(column, [((0, 1, 0), (0, 0, 0))])
+    row3 = send(column, [((0, 3, 0), (0, 0, 0))])
+    row2 = send(pass_on, [((0, 1, 0), (0, 0, 0))])
+    z2 = sends(after(z1, *lists, row1, row3), along_z)
+    y1 = sends(lists[:2], along_y)
+    y1 += sends(after(lists[2:], *z2, row2), along_y)
+    z3 = sends(z2, along_z)
+    y2 = sends(y1[:2], along_y)
+    y1_other = sends(y1, swap)
+    z4 = sends(after(z3, *y1)[:2], along_z)
+    y2_other = sends(y2, swap)
+    z3_other = sends(z3, swap)
+    roots = [(2 * ROOT + 2 * i, 0, 6, x) for i, x in enumerate((column, row1, row2, row3))]
+    spans = near_spans + pieces_of(YN1, NY_CUT, y1, y1_other) + pieces_of(YN2, NY_CUT[:3], y2, y2_other) + roots
+    base = add_up(where, end, codes, jnp.zeros((8, 128), F32), spans, BUF, YN2, "sum_near")
+    z4_other = sends(z4, swap)
+    spans = pieces_of(ZF3, FZ_CUT, z3, z3_other) + pieces_of(ZF4, FZ_CUT[:3], z4, z4_other)
+    return add_up(where, end, codes, base, spans, ZF3, ZF4, "sum_far")
+
+
 def local(front, pivot_tiles, send_table):
     place = lax.axis_index("front").astype(jnp.int32)
+    leaf = lax.axis_index("leaf").astype(jnp.int32)
+    where = jnp.stack([leaf // 8, (leaf // 2) % 4, leaf % 2])
+    table = send_table[0, 0]
+    used = table[0] >= 0
+    tile = jnp.where(used, table[0] * 7 + table[1] - 1, -1)
+    code = jnp.where(used, tile * 16 + table[2], -1)
+    wide = jnp.pad(code.astype(F32).reshape(1, 64), ((0, 7), (0, 64)))
+    codes = lax.all_gather(wide, "leaf")[:, 0, :64].reshape(32, 128).astype(jnp.int32)
     up = [(i, (i + 1) % 4) for i in range(4)]
     down = [(i, (i - 1) % 4) for i in range(4)]
     own = [[front[0, r, 0, :, k * T:k * T + T].astype(F32) for k in range(2)] for r in range(2)]
     from_left = [[None, None], [None, None]]
     from_right = [[None, None], [None, None]]
     from_far = [[None, None], [None, None]]
-    for r in range(2):
-        for k in range(2):
-            from_left[r][k] = lax.ppermute(own[r][k], "front", up)
-            from_right[r][k] = lax.ppermute(own[r][k], "front", down)
-            if k == 0:
-                from_far[r][k] = lax.ppermute(from_left[r][k], "front", up)
-            else:
-                from_far[r][k] = lax.ppermute(from_right[r][k], "front", down)
+    from_left[0][0] = lax.ppermute(own[0][0], "front", up)
+    from_right[0][0] = lax.ppermute(own[0][0], "front", down)
+    from_far[0][0] = lax.ppermute(from_left[0][0], "front", up)
+    from_right[0][1] = lax.ppermute(tie(own[0][1], from_left[0][0], from_right[0][0]), "front", down)
+    from_left[0][1] = lax.ppermute(tie(own[0][1], from_far[0][0]), "front", up)
+    from_far[0][1] = lax.ppermute(from_right[0][1], "front", down)
+    for k in range(2):
+        from_left[1][k] = lax.ppermute(tie(own[1][k], from_far[0][0]), "front", up)
+        from_right[1][k] = lax.ppermute(tie(own[1][k], from_far[0][0]), "front", down)
+    from_far[1][0] = lax.ppermute(from_left[1][0], "front", up)
+    from_far[1][1] = lax.ppermute(from_right[1][1], "front", down)
     by_q = [own, from_right, from_far, from_left]
 
-    def of_owner(owner, r, k):
+    def of_owner(owner, r, k, *after):
         q = lax.rem(owner - place + 4, 4)
+        if after:
+            q = tie(q, *after)
         out = by_q[0][r][k]
         for i in range(1, 4):
             out = jnp.where(q == i, by_q[i][r][k], out)
@@ -227,6 +591,18 @@
         compiler_params=pltpu.CompilerParams(vmem_limit_bytes=16 << 20),
         name="first",
     )(of_owner(0, 0, 0))
+    *tables, over = pl.pallas_call(
+        plan_kernel,
+        out_shape=tuple(jax.ShapeDtypeStruct((n, 128), jnp.int32) for n in (1, 1, 32, 32, 32)) + (jax.ShapeDtypeStruct((1, 1), F32),),
+        in_specs=[SMEM, VMEM],
+        out_specs=(VMEM,) * 6,
+        name="plan",
+    )(where, tie(codes, inv0))
+    over = jnp.maximum(over, tie(lax.ppermute(over, "front", up), inv0))
+    across = lax.ppermute(over, "front", [(i, (i + 2) % 4) for i in range(4)])
+
+    w10 = of_owner(1, 0, 0, inv0)
+    w11 = of_owner(1, 0, 1, inv0)
     l10, inv1 = pl.pallas_call(
         second_kernel,
         out_shape=(jax.ShapeDtypeStruct((T, T), F32),) * 2,
@@ -235,38 +611,20 @@
         scratch_shapes=[pltpu.VMEM((B, 128), F32)],
         compiler_params=pltpu.CompilerParams(vmem_limit_bytes=16 << 20),
         name="second",
-    )(pivot_tiles, inv0, of_owner(1, 0, 0), of_owner(1, 0, 1))
-
-    table = send_table[0, 0]
-    where = jnp.where(table[0] >= 0, table[0] * 8 + table[1], -1)
-    ids = jnp.arange(64, dtype=jnp.int32)
-    slots = jnp.max(jnp.where(where[None, :] == jnp.arange(16, dtype=jnp.int32)[:, None], ids[None, :], -1), axis=1)
+    )(pivot_tiles, inv0, w10, w11)
+
     received = [by_q[q][r][k] for q in range(1, 4) for r in range(2) for k in range(2)]
-    factor, outgoing = pl.pallas_call(
+    factor, work, zero = pl.pallas_call(
         panel_kernel,
-        out_shape=(jax.ShapeDtypeStruct((1, 2, 1, T, 2 * T), F32), jax.ShapeDtypeStruct((64, T, T), F32)),
+        out_shape=(jax.ShapeDtypeStruct((1, 2, 1, T, 2 * T), F32),) + tiles(TILES) + (jax.ShapeDtypeStruct((T, T), F32),),
         in_specs=[SMEM, SMEM] + [VMEM] * 16,
-        out_specs=(VMEM, ANY),
-        scratch_shapes=[
-            pltpu.VMEM((8, T, 2 * T), BF16),
-            pltpu.VMEM((8, T, 2 * T), BF16),
-            pltpu.VMEM((16, T, T), F32),
-            pltpu.SemaphoreType.DMA((16,)),
-        ],
+        out_specs=(VMEM, VMEM, VMEM),
+        scratch_shapes=[pltpu.VMEM((8, T, 2 * T), BF16), pltpu.VMEM((8, T, 2 * T), BF16)],
         compiler_params=pltpu.CompilerParams(vmem_limit_bytes=40 << 20),
         name="panel",
-    )(place.reshape(1), slots, inv0, l10, inv1, front, *received)
-    arrived = lax.all_to_all(outgoing, "leaf", split_axis=0, concat_axis=0, tiled=True)
-    targets = lax.all_to_all(table[2], "leaf", split_axis=0, concat_axis=0, tiled=True)
-    ancestor = pl.pallas_call(
-        add_kernel,
-        out_shape=jax.ShapeDtypeStruct((ASLOT, T, T), F32),
-        grid=(16,),
-        in_specs=[SMEM, pl.BlockSpec((4, T, T), lambda i: (i, 0, 0))],
-        out_specs=pl.BlockSpec((ASLOT, T, T), lambda i: (0, 0, 0)),
-        compiler_params=pltpu.CompilerParams(vmem_limit_bytes=32 << 20),
-        name="add",
-    )(targets, arrived)
+    )(place.reshape(1), tile[0:1], inv0, l10, inv1, front, *received)
+    over = jnp.maximum(over, tie(across, zero))
+    ancestor = lax.cond(over[0, 0] > 0.0, dense, sparse, work, zero, tile, table[2], codes, where, *tables)
     return (factor, ancestor.reshape(1, 1, ASLOT, T, T))
 
 

time: 476 us -> 476 us (level)
  the two profiles are of different devices: /device:TPU:49 before, /device:TPU:6 now
where the time goes in v2:
time: 476 us; the launch traced here: 467 us
  waiting for transfers between devices  225 us (47%)
  starting transfers between devices  89.8 us (19%)
  Pallas kernels  80 us (17%)
  blocking collectives  47.2 us (10%)
  local copies, waits for them, and re-layouts  14.8 us (3%)
    ppermute x53, waiting for transfers between devices, send(): lax.ppermute(x, 'leaf', [(leaf_id(*a), leaf_id(*b)) for a, b in pairs])  208 us
    ppermute x53, starting transfers between devices, send(): lax.ppermute(x, 'leaf', [(leaf_id(*a), leaf_id(*b)) for a, b in pairs])  62 us
    all_gather x1, blocking collectives, local(): lax.all_gather(wide, 'leaf')[:, 0, :64].reshape(32, 128).astype(jnp.int32)  47.2 us
    pallas_call x4, Pallas kernels, gather(): pl.pallas_call(lambda *refs: gather_kernel([span[:3] for span in spans],...  28.5 us
    pallas_call x2, Pallas kernels, add_up(): pl.pallas_call(lambda *refs: sum_kernel([span[:3] for span in spans], fir...  23.3 us
    cond x53, local copies, waits for them, and re-layouts  14 us
    pallas_call x1, Pallas kernels, local(): pl.pallas_call(panel_kernel, out_shape=(jax.ShapeDtypeStruct((1, 2, 1, T,...  13.5 us
    pallas_call x1, Pallas kernels, local(): pl.pallas_call(first_kernel, out_shape=jax.ShapeDtypeStruct((T, T), F32),...  12.1 us
  transfers between devices with their start and end apart: 67, of which 28 were waited for; matrix products, arithmetic and copies ran while one was open for 1% of the time, Pallas kernels for 14%

profile of v2, /device:TPU:6, one launch (start us, length us, event | category | flops | bytes accessed | tf_op | source)
XLA Modules:
  0.0 466.9 jit_solution(14085129171947126501)
XLA Ops:
  6.4 4.5 collective-permute-done.53.refs_8_
  12.6 3.2 collective-permute-start.54
  16.5 3.3 collective-permute-done.54.refs_4_
  19.8 3.7 collective-permute-start.56
  23.5 3.2 collective-permute-start.61
  26.8 47.2 %all-gather = f32[512,128]{1,0:T(8,128)S(1)} all-gather(f32[8,128]{1,0:T(8,128)S(1)} %pad.4), channel_id=2, replica_groups=mesh['leaf'=64,'front'=4] {'leaf'}, dimensions={0}, use_global_device_ids=true | all-gather | bytes 266240 | tf_op jit(solution)/shard_map/all_gather | solution.py:556
  74.8 12.1 %first.1.inv0_ref = f32[256,256]{1,0:T(8,128)S(1)} custom-call(f32[256,256]{1,0:T(8,128)S(1)} %select_select_fusion.2.w00_ref), custom_call_target="tpu_custom_call" | custom-call | tf_op jit(solution)/shard_map/first/pallas_call | solution.py:585
  89.2 3.2 collective-permute-start.65
  95.2 4.0 collective-permute-start.64
  99.2 2.9 collective-permute-start.66
  102.0 5.4 %collective-permute-start.62 = (f32[256,256]{1,0:T(8,128)}, f32[256,256]{1,0:T(8,128)S(1)}, u32[]{:S(2)}, u32[]{:S(2)}) collective-permute-start(f32[256,256]{1,0:T(8,128)} %collective-permute-done.61.refs_10_), channel_id=1, source_target_pairs={{0,1},{1,2},{2,3},{3,0},{4,5},{5,6},{6,7},{7,4},{8,9},{9,10},{10,1... | collective-permute-start | bytes 786440 | tf_op jit(solution)/shard_map/ppermute | solution.py:572
  108.9 2.7 collective-permute-done.62.refs_6_
  111.6 3.6 collective-permute-done.63.refs_7_
  115.2 13.5 %panel.1 = (f32[1,2,1,256,512]{4,3,2,1,0:T(8,128)}, f32[14,256,256]{2,1,0:T(8,128)}, f32[256,256]{1,0:T(8,128)S(1)}) custom-call(s32[1]{0:T(128)} %bitcast.10.place_ref, s32[1]{0:T(128)S(1)} %bitcast.89, f32[256,256]{1,0:T(8,128)S(1)} %first.1.inv0_ref, f32[256,256]{1,0:T(8,128)S(1)} %get-tuple-element.99.l10_ref, ...), custom_call_target="tpu_custom_call" | custom-call | tf_op jit(solution)/shard_map/panel/pallas_call | solution.py:617
  129.4 336.5 %conditional.1 = (f32[1,1,16,256,256]{4,3,2,1,0:T(8,128)}) conditional(s32[]{:T(128)} %bitcast.26, (f32[14,256,256]{2,1,0:T(8,128)}, s32[3]{0:T(128)S(1)}, s32[1,128]{1,0:T(1,128)S(1)}, s32[1,128]{1,0:T(1,128)S(1)}, s32[32,128]{1,0:T(8,128)S(1)}, /*index=5*/s32[32,128]{1,0:T(8,128)S(1)}, f32[256,256]{1,0:T(8,128)S(1)}, s32[32,128]{1,0:T(8,128)S(1)}, ...), branch_computations={%region_0.1_spmd, %region_1.2_spmd} | conditional | bytes 380639776 | solution.py:627
  129.7 6.6 %collective-permute-done.refs_3_.refs_5_ = f32[14,256,256]{2,1,0:T(8,128)S(1)} collective-permute-done((f32[14,256,256]{2,1,0:T(8,128)}, f32[14,256,256]{2,1,0:T(8,128)S(1)}, u32[]{:S(2)}, u32[]{:S(2)}) %collective-permute-start) | collective-permute-done | bytes 3670048 | tf_op jit(solution)/shard_map/cond/branch_0_fun/ppermute | solution.py:465
  136.3 4.6 queue.1
  140.9 4.3 queue_far.1
  145.2 7.4 %collective-permute-start.7 = (f32[6,256,256]{2,1,0:T(8,128)S(1)}, f32[6,256,256]{2,1,0:T(8,128)S(1)}, u32[]{:S(2)}, u32[]{:S(2)}) collective-permute-start(f32[6,256,256]{2,1,0:T(8,128)S(1)} %get-tuple-element.43), channel_id=1, source_target_pairs={{0,8},{4,28},{8,16},{12,4},{16,24},{20,12},{24,0},{28,20},{32,40},... | collective-permute-start | bytes 4718600 | tf_op jit(solution)/shard_map/cond/branch_0_fun/ppermute | solution.py:465
  152.6 3.0 collective-permute-start.3
  155.8 23.2 %collective-permute-done.8.refs_5_ = f32[3,256,256]{2,1,0:T(8,128)S(1)} collective-permute-done((f32[3,256,256]{2,1,0:T(8,128)S(1)}, f32[3,256,256]{2,1,0:T(8,128)S(1)}, u32[]{:S(2)}, u32[]{:S(2)}) %collective-permute-start.8) | collective-permute-done | bytes 786464 | tf_op jit(solution)/shard_map/cond/branch_0_fun/ppermute | solution.py:465
  179.0 2.5 collective-permute-start.17
  181.5 4.0 collective-permute-done.2.refs_5_.refs_7_
  185.5 14.0 %collective-permute-done.3.refs_6_.refs_8_ = f32[5,256,256]{2,1,0:T(8,128)S(1)} collective-permute-done((f32[5,256,256]{2,1,0:T(8,128)S(1)}, f32[5,256,256]{2,1,0:T(8,128)S(1)}, u32[]{:S(2)}, u32[]{:S(2)}) %collective-permute-start.3) | collective-permute-done | bytes 1310752 | tf_op jit(solution)/shard_map/cond/branch_0_fun/ppermute | solution.py:465
  202.1 10.3 %collective-permute-done.22 = f32[256,256]{1,0:T(8,128)S(1)} collective-permute-done((f32[256,256]{1,0:T(8,128)S(1)}, f32[256,256]{1,0:T(8,128)S(1)}, u32[]{:S(2)}, u32[]{:S(2)}) %collective-permute-start.22) | collective-permute-done | bytes 262176 | tf_op jit(solution)/shard_map/cond/branch_0_fun/ppermute | solution.py:465
  213.7 21.0 %collective-permute-done.23 = f32[256,256]{1,0:T(8,128)S(1)} collective-permute-done((f32[256,256]{1,0:T(8,128)S(1)}, f32[256,256]{1,0:T(8,128)S(1)}, u32[]{:S(2)}, u32[]{:S(2)}) %collective-permute-start.23) | collective-permute-done | bytes 262176 | tf_op jit(solution)/shard_map/cond/branch_0_fun/ppermute | solution.py:465
  236.1 10.2 %collective-permute-done.25 = f32[256,256]{1,0:T(8,128)S(1)} collective-permute-done((f32[256,256]{1,0:T(8,128)S(1)}, f32[256,256]{1,0:T(8,128)S(1)}, u32[]{:S(2)}, u32[]{:S(2)}) %collective-permute-start.25) | collective-permute-done | bytes 262176 | tf_op jit(solution)/shard_map/cond/branch_0_fun/ppermute | solution.py:465
  247.6 10.1 %collective-permute-done.26 = f32[256,256]{1,0:T(8,128)S(1)} collective-permute-done((f32[256,256]{1,0:T(8,128)S(1)}, f32[256,256]{1,0:T(8,128)S(1)}, u32[]{:S(2)}, u32[]{:S(2)}) %collective-permute-start.26) | collective-permute-done | bytes 262176 | tf_op jit(solution)/shard_map/cond/branch_0_fun/ppermute | solution.py:465
  259.0 9.5 %collective-permute-done.27 = f32[256,256]{1,0:T(8,128)S(1)} collective-permute-done((f32[256,256]{1,0:T(8,128)S(1)}, f32[256,256]{1,0:T(8,128)S(1)}, u32[]{:S(2)}, u32[]{:S(2)}) %collective-permute-start.27) | collective-permute-done | bytes 262176 | tf_op jit(solution)/shard_map/cond/branch_0_fun/ppermute | solution.py:465
  273.5 4.0 collective-permute-done.6.refs_9_.refs_11_
  281.1 9.6 %turn_far.1 = (f32[4,256,256]{2,1,0:T(8,128)S(1)}, f32[3,256,256]{2,1,0:T(8,128)S(1)}, f32[3,256,256]{2,1,0:T(8,128)S(1)}) custom-call(s32[3]{0:T(128)S(1)} %get-tuple-element.29.refs_0_, s32[32,128]{1,0:T(8,128)S(1)} %get-tuple-element.51.refs_1_, f32[14,256,256]{2,1,0:T(8,128)} %get-tuple-element.32.refs_2_.refs_4_, ...), custom_call_target="tpu_custom_call" | custom-call | tf_op jit(solution)/shard_map/cond/branch_0_fun/turn_far/pallas_call | solution.py:342
  290.8 9.9 %turn_near.1 = (f32[6,256,256]{2,1,0:T(8,128)S(1)}, f32[6,256,256]{2,1,0:T(8,128)S(1)}, f32[6,256,256]{2,1,0:T(8,128)S(1)}) custom-call(s32[3]{0:T(128)S(1)} %get-tuple-element.29.refs_0_, s32[32,128]{1,0:T(8,128)S(1)} %get-tuple-element.47.refs_1_, f32[14,256,256]{2,1,0:T(8,128)} %get-tuple-element.32.refs_2_.refs_4_, ...), custom_call_target="tpu_custom_call" | custom-call | tf_op jit(solution)/shard_map/cond/branch_0_fun/turn_near/pallas_call | solution.py:342
  301.0 2.4 collective-permute-start.14
  304.9 24.3 %collective-permute-done.21 = f32[3,256,256]{2,1,0:T(8,128)S(1)} collective-permute-done((f32[3,256,256]{2,1,0:T(8,128)S(1)}, f32[3,256,256]{2,1,0:T(8,128)S(1)}, u32[]{:S(2)}, u32[]{:S(2)}) %collective-permute-start.21) | collective-permute-done | bytes 786464 | tf_op jit(solution)/shard_map/cond/branch_0_fun/ppermute | solution.py:465
  329.2 3.1 collective-permute-start.39
  332.3 7.9 %collective-permute-done.14.refs_17_ = f32[6,256,256]{2,1,0:T(8,128)S(1)} collective-permute-done((f32[6,256,256]{2,1,0:T(8,128)S(1)}, f32[6,256,256]{2,1,0:T(8,128)S(1)}, u32[]{:S(2)}, u32[]{:S(2)}) %collective-permute-start.14) | collective-permute-done | bytes 1572896 | tf_op jit(solution)/shard_map/cond/branch_0_fun/ppermute | solution.py:465
  340.2 2.7 collective-permute-done.34.refs_28_
  343.0 13.8 %collective-permute-done.31 = f32[3,256,256]{2,1,0:T(8,128)S(1)} collective-permute-done((f32[3,256,256]{2,1,0:T(8,128)S(1)}, f32[3,256,256]{2,1,0:T(8,128)S(1)}, u32[]{:S(2)}, u32[]{:S(2)}) %collective-permute-start.31) | collective-permute-done | bytes 786464 | tf_op jit(solution)/shard_map/cond/branch_0_fun/ppermute | solution.py:465
  356.8 8.4 %collective-permute-done.32 = f32[3,256,256]{2,1,0:T(8,128)S(1)} collective-permute-done((f32[3,256,256]{2,1,0:T(8,128)S(1)}, f32[3,256,256]{2,1,0:T(8,128)S(1)}, u32[]{:S(2)}, u32[]{:S(2)}) %collective-permute-start.32) | collective-permute-done | bytes 786464 | tf_op jit(solution)/shard_map/cond/branch_0_fun/ppermute | solution.py:465
  365.3 7.6 %collective-permute-start.36 = (f32[6,256,256]{2,1,0:T(8,128)S(1)}, f32[6,256,256]{2,1,0:T(8,128)S(1)}, u32[]{:S(2)}, u32[]{:S(2)}) collective-permute-start(f32[6,256,256]{2,1,0:T(8,128)S(1)} %collective-permute-done.13.refs_16_), channel_id=1, source_target_pairs={{0,4},{4,0},{8,12},{12,8},{16,20},{20,16},{24,28},{28,24},{32,36},... | collective-permute-start | bytes 4718600 | tf_op jit(solution)/shard_map/cond/branch_0_fun/ppermute | solution.py:465
  373.9 13.2 %collective-permute-start.37 = (f32[6,256,256]{2,1,0:T(8,128)S(1)}, f32[6,256,256]{2,1,0:T(8,128)S(1)}, u32[]{:S(2)}, u32[]{:S(2)}) collective-permute-start(f32[6,256,256]{2,1,0:T(8,128)S(1)} %collective-permute-done.14.refs_17_), channel_id=1, source_target_pairs={{0,4},{4,0},{8,12},{12,8},{16,20},{20,16},{24,28},{28,24},{32,36},... | collective-permute-start | bytes 4718600 | tf_op jit(solution)/shard_map/cond/branch_0_fun/ppermute | solution.py:465
  387.1 10.6 %collective-permute-done.45.refs_6_ = f32[3,256,256]{2,1,0:T(8,128)S(1)} collective-permute-done((f32[3,256,256]{2,1,0:T(8,128)S(1)}, f32[3,256,256]{2,1,0:T(8,128)S(1)}, u32[]{:S(2)}, u32[]{:S(2)}) %collective-permute-start.45) | collective-permute-done | bytes 786464 | tf_op jit(solution)/shard_map/cond/branch_0_fun/ppermute | solution.py:465
  397.7 3.0 collective-permute-start.41
  400.7 2.8 collective-permute-start.38
  404.1 15.5 %collective-permute-done.49.refs_10_ = f32[4,256,256]{2,1,0:T(8,128)S(1)} collective-permute-done((f32[4,256,256]{2,1,0:T(8,128)S(1)}, f32[4,256,256]{2,1,0:T(8,128)S(1)}, u32[]{:S(2)}, u32[]{:S(2)}) %collective-permute-start.49) | collective-permute-done | bytes 1048608 | tf_op jit(solution)/shard_map/cond/branch_0_fun/ppermute | solution.py:465
  420.2 7.8 %collective-permute-done.50.refs_11_ = f32[3,256,256]{2,1,0:T(8,128)S(1)} collective-permute-done((f32[3,256,256]{2,1,0:T(8,128)S(1)}, f32[3,256,256]{2,1,0:T(8,128)S(1)}, u32[]{:S(2)}, u32[]{:S(2)}) %collective-permute-start.50) | collective-permute-done | bytes 786464 | tf_op jit(solution)/shard_map/cond/branch_0_fun/ppermute | solution.py:465
  428.5 18.2 %sum_near.1.refs_3_ = f32[16,256,256]{2,1,0:T(8,128)} custom-call(s32[3]{0:T(128)S(1)} %get-tuple-element.29.refs_0_, s32[32,128]{1,0:T(8,128)S(1)} %get-tuple-element.30.refs_1_, s32[32,128]{1,0:T(8,128)S(1)} %get-tuple-element.31.refs_2_, f32[8,128]{1,0:T(8,128)S(1)} %broadcast_1_refs_3_.0.refs_3_, f32[14,256,256]{2,1,0:T(8,128)} %get-tuple-element.32.refs_2_.refs_4_, ...), custom_call_target="tpu_custom_call" | custom-call | tf_op jit(solution)/shard_map/cond/branch_0_fun/sum_near/pallas_call | solution.py:408
  460.7 5.0 %sum_far.1 = f32[16,256,256]{2,1,0:T(8,128)} custom-call(s32[3]{0:T(128)S(1)} %get-tuple-element.29.refs_0_, s32[32,128]{1,0:T(8,128)S(1)} %get-tuple-element.30.refs_1_, s32[32,128]{1,0:T(8,128)S(1)} %get-tuple-element.31.refs_2_, f32[16,256,256]{2,1,0:T(8,128)S(1)} %copy-done.1, f32[4,256,256]{2,1,0:T(8,128)S(1)} %collective-permute-done.43.refs_4_, ...), custom_call_target="tpu_custom_call" | custom-call | tf_op jit(solution)/shard_map/cond/branch_0_fun/sum_far/pallas_call | solution.py:408
  (166 shorter events, 48.9 us)
Async XLA Ops:
  12.6 14.2 %collective-permute-start.57 = (f32[256,256]{1,0:T(8,128)}, f32[256,256]{1,0:T(8,128)S(1)}, u32[]{:S(2)}, u32[]{:S(2)}) collective-permute-start(f32[256,256]{1,0:T(8,128)} %get-tuple-element.98), channel_id=1, source_target_pairs={{0,3},{1,0},{2,1},{3,2},{4,7},{5,4},{6,5},{7,6},{8,11},{9,8},{10,9... | collective-permute-start | bytes 786440 | tf_op jit(solution)/shard_map/ppermute | solution.py:566
  19.8 75.4 %collective-permute-start.56 = (f32[256,256]{1,0:T(8,128)}, f32[256,256]{1,0:T(8,128)}, u32[]{:S(2)}, u32[]{:S(2)}) collective-permute-start(f32[256,256]{1,0:T(8,128)} %get-tuple-element.98), channel_id=1, source_target_pairs={{0,1},{1,2},{2,3},{3,0},{4,5},{5,6},{6,7},{7,4},{8,9},{9,10},{10,1... | collective-permute-start | bytes 786440 | tf_op jit(solution)/shard_map/ppermute | solution.py:567
  23.5 83.9 %collective-permute-start.60 = (f32[256,256]{1,0:T(8,128)}, f32[256,256]{1,0:T(8,128)}, u32[]{:S(2)}, u32[]{:S(2)}) collective-permute-start(f32[256,256]{1,0:T(8,128)} %get-tuple-element.102), channel_id=1, source_target_pairs={{0,3},{1,0},{2,1},{3,2},{4,7},{5,4},{6,5},{7,6},{8,11},{9,8},{10,9... | collective-permute-start | bytes 786440 | tf_op jit(solution)/shard_map/ppermute | solution.py:571
  23.5 78.5 %collective-permute-start.61 = (f32[256,256]{1,0:T(8,128)}, f32[256,256]{1,0:T(8,128)}, u32[]{:S(2)}, u32[]{:S(2)}) collective-permute-start(f32[256,256]{1,0:T(8,128)} %get-tuple-element.101), channel_id=1, source_target_pairs={{0,1},{1,2},{2,3},{3,0},{4,5},{5,6},{6,7},{7,4},{8,9},{9,10},{10,1... | collective-permute-start | bytes 786440 | tf_op jit(solution)/shard_map/ppermute | solution.py:570
  26.8 72.4 %collective-permute-start.58 = (f32[256,256]{1,0:T(8,128)S(1)}, f32[256,256]{1,0:T(8,128)}, u32[]{:S(2)}, u32[]{:S(2)}) collective-permute-start(f32[256,256]{1,0:T(8,128)S(1)} %collective-permute-done.57.refs_1_), channel_id=1, source_target_pairs={{0,3},{1,0},{2,1},{3,2},{4,7},{5,4},{6,5},{7,6},{8,11},{9,8},{10,9... | collective-permute-start | bytes 786440 | tf_op jit(solution)/shard_map/ppermute | solution.py:568
  94.0 15.0 %collective-permute-start.59 = (f32[256,256]{1,0:T(8,128)}, f32[256,256]{1,0:T(8,128)S(1)}, u32[]{:S(2)}, u32[]{:S(2)}) collective-permute-start(f32[256,256]{1,0:T(8,128)} %get-tuple-element.101), channel_id=1, source_target_pairs={{0,3},{1,0},{2,1},{3,2},{4,7},{5,4},{6,5},{7,6},{8,11},{9,8},{10,9... | collective-permute-start | bytes 786440 | tf_op jit(solution)/shard_map/ppermute | solution.py:571
  99.2 29.5 %collective-permute-start.66 = (f32[1,1]{1,0:T(1,128)}, f32[1,1]{1,0:T(1,128)}, u32[]{:S(2)}, u32[]{:S(2)}) collective-permute-start(f32[1,1]{1,0:T(1,128)} %max.6), channel_id=1, source_target_pairs={{0,2},{1,3},{2,0},{3,1},{4,6},{5,7},{6,4},{7,5},{8,10},{9,11},{10,... | collective-permute-start | bytes 20 | tf_op jit(solution)/shard_map/ppermute | solution.py:602
  145.2 33.7 %collective-permute-start.7 = (f32[6,256,256]{2,1,0:T(8,128)S(1)}, f32[6,256,256]{2,1,0:T(8,128)S(1)}, u32[]{:S(2)}, u32[]{:S(2)}) collective-permute-start(f32[6,256,256]{2,1,0:T(8,128)S(1)} %get-tuple-element.43), channel_id=1, source_target_pairs={{0,8},{4,28},{8,16},{12,4},{16,24},{20,12},{24,0},{28,20},{32,40},... | collective-permute-start | bytes 4718600 | tf_op jit(solution)/shard_map/cond/branch_0_fun/ppermute | solution.py:465
  152.6 28.9 %collective-permute-start.1 = (f32[5,256,256]{2,1,0:T(8,128)S(1)}, f32[5,256,256]{2,1,0:T(8,128)S(1)}, u32[]{:S(2)}, u32[]{:S(2)}) collective-permute-start(f32[5,256,256]{2,1,0:T(8,128)S(1)} %get-tuple-element.40), channel_id=1, source_target_pairs={{0,32},{4,228},{8,40},{12,236},{16,48},{20,244},{24,56},{28,252},{... | collective-permute-start | bytes 3932168 | tf_op jit(solution)/shard_map/cond/branch_0_fun/ppermute | solution.py:465
  152.6 32.9 %collective-permute-start.2 = (f32[5,256,256]{2,1,0:T(8,128)S(1)}, f32[5,256,256]{2,1,0:T(8,128)S(1)}, u32[]{:S(2)}, u32[]{:S(2)}) collective-permute-start(f32[5,256,256]{2,1,0:T(8,128)S(1)} %get-tuple-element.41), channel_id=1, source_target_pairs={{0,32},{4,228},{8,40},{12,236},{16,48},{20,244},{24,56},{28,252},{... | collective-permute-start | bytes 3932168 | tf_op jit(solution)/shard_map/cond/branch_0_fun/ppermute | solution.py:465
  152.6 46.9 %collective-permute-start.3 = (f32[5,256,256]{2,1,0:T(8,128)S(1)}, f32[5,256,256]{2,1,0:T(8,128)S(1)}, u32[]{:S(2)}, u32[]{:S(2)}) collective-permute-start(f32[5,256,256]{2,1,0:T(8,128)S(1)} %get-tuple-element.42), channel_id=1, source_target_pairs={{0,32},{4,228},{8,40},{12,236},{16,48},{20,244},{24,56},{28,252},{... | collective-permute-start | bytes 3932168 | tf_op jit(solution)/shard_map/cond/branch_0_fun/ppermute | solution.py:465
  155.7 23.3 %collective-permute-start.8 = (f32[3,256,256]{2,1,0:T(8,128)S(1)}, f32[3,256,256]{2,1,0:T(8,128)S(1)}, u32[]{:S(2)}, u32[]{:S(2)}) collective-permute-start(f32[3,256,256]{2,1,0:T(8,128)S(1)} %get-tuple-element.44), channel_id=1, source_target_pairs={{0,8},{4,28},{8,16},{12,4},{16,24},{20,12},{24,0},{28,20},{32,40},... | collective-permute-start | bytes 2359304 | tf_op jit(solution)/shard_map/cond/branch_0_fun/ppermute | solution.py:465
  179.0 90.6 %collective-permute-start.17 = (f32[6,256,256]{2,1,0:T(8,128)S(1)}, f32[6,256,256]{2,1,0:T(8,128)S(1)}, u32[]{:S(2)}, u32[]{:S(2)}) collective-permute-start(f32[6,256,256]{2,1,0:T(8,128)S(1)} %collective-permute-done.7.refs_4_), channel_id=1, source_target_pairs={{0,8},{4,28},{8,16},{12,4},{16,24},{20,12},{24,0},{28,20},{32,40},... | collective-permute-start | bytes 4718600 | tf_op jit(solution)/shard_map/cond/branch_0_fun/ppermute | solution.py:465
  199.5 69.0 %collective-permute-start.9 = (f32[5,256,256]{2,1,0:T(8,128)S(1)}, f32[5,256,256]{2,1,0:T(8,128)S(1)}, u32[]{:S(2)}, u32[]{:S(2)}) collective-permute-start(f32[5,256,256]{2,1,0:T(8,128)S(1)} %collective-permute-done.1.refs_4_.refs_6_), channel_id=1, source_target_pairs={{0,32},{4,228},{8,40},{12,236},{16,48},{20,244},{24,56},{28,252},{... | collective-permute-start | bytes 3932168 | tf_op jit(solution)/shard_map/cond/branch_0_fun/ppermute | solution.py:465
  199.5 69.5 %collective-permute-start.10 = (f32[5,256,256]{2,1,0:T(8,128)S(1)}, f32[5,256,256]{2,1,0:T(8,128)S(1)}, u32[]{:S(2)}, u32[]{:S(2)}) collective-permute-start(f32[5,256,256]{2,1,0:T(8,128)S(1)} %collective-permute-done.2.refs_5_.refs_7_), channel_id=1, source_target_pairs={{0,32},{4,228},{8,40},{12,236},{16,48},{20,244},{24,56},{28,252},{... | collective-permute-start | bytes 3932168 | tf_op jit(solution)/shard_map/cond/branch_0_fun/ppermute | solution.py:465
  200.8 33.9 %collective-permute-start.23 = (f32[256,256]{1,0:T(8,128)S(1)}, f32[256,256]{1,0:T(8,128)S(1)}, u32[]{:S(2)}, u32[]{:S(2)}) collective-permute-start(f32[256,256]{1,0:T(8,128)S(1)} %get-tuple-element.59), channel_id=1, source_target_pairs={{100,0},{108,8},{116,16},{124,24},{101,1},{109,9},{117,17},{125,25... | collective-permute-start | bytes 786440 | tf_op jit(solution)/shard_map/cond/branch_0_fun/ppermute | solution.py:465
  212.5 23.6 %collective-permute-start.24 = (f32[256,256]{1,0:T(8,128)S(1)}, f32[256,256]{1,0:T(8,128)S(1)}, u32[]{:S(2)}, u32[]{:S(2)}) collective-permute-start(f32[256,256]{1,0:T(8,128)S(1)} %get-tuple-element.59), channel_id=1, source_target_pairs={{128,0},{136,8},{144,16},{152,24},{129,1},{137,9},{145,17},{153,25... | collective-permute-start | bytes 786440 | tf_op jit(solution)/shard_map/cond/branch_0_fun/ppermute | solution.py:465
  236.0 33.1 %collective-permute-start.16 = (f32[3,256,256]{2,1,0:T(8,128)S(1)}, f32[3,256,256]{2,1,0:T(8,128)S(1)}, u32[]{:S(2)}, u32[]{:S(2)}) collective-permute-start(f32[3,256,256]{2,1,0:T(8,128)S(1)} %collective-permute-done.8.refs_5_), channel_id=1, source_target_pairs={{0,4},{4,0},{8,12},{12,8},{16,20},{20,16},{24,28},{28,24},{32,36},... | collective-permute-start | bytes 2359304 | tf_op jit(solution)/shard_map/cond/branch_0_fun/ppermute | solution.py:465
  271.5 29.5 %collective-permute-start.28 = (f32[6,256,256]{2,1,0:T(8,128)S(1)}, f32[6,256,256]{2,1,0:T(8,128)S(1)}, u32[]{:S(2)}, u32[]{:S(2)}) collective-permute-start(f32[6,256,256]{2,1,0:T(8,128)S(1)} %bitcast_dynamic-update-slice_fusion.refs_26_), channel_id=1, source_target_pairs={{8,0},{9,1},{10,2},{11,3}} | collective-permute-start | bytes 4718600 | tf_op jit(solution)/shard_map/cond/branch_0_fun/ppermute | solution.py:465
  273.4 17.3 %collective-permute-start.11 = (f32[5,256,256]{2,1,0:T(8,128)S(1)}, f32[5,256,256]{2,1,0:T(8,128)S(1)}, u32[]{:S(2)}, u32[]{:S(2)}) collective-permute-start(f32[5,256,256]{2,1,0:T(8,128)S(1)} %collective-permute-done.9.refs_10_.refs_12_), channel_id=1, source_target_pairs={{0,4},{4,0},{8,12},{12,8},{16,20},{20,16},{24,28},{28,24},{32,36},... | collective-permute-start | bytes 3932168 | tf_op jit(solution)/shard_map/cond/branch_0_fun/ppermute | solution.py:465
  277.7 25.8 %collective-permute-start.33 = (f32[6,256,256]{2,1,0:T(8,128)S(1)}, f32[6,256,256]{2,1,0:T(8,128)S(1)}, u32[]{:S(2)}, u32[]{:S(2)}) collective-permute-start(f32[6,256,256]{2,1,0:T(8,128)S(1)} %bitcast_dynamic-update-slice_fusion.refs_26_), channel_id=1, source_target_pairs={{16,8},{17,9},{18,10},{19,11}} | collective-permute-start | bytes 4718600 | tf_op jit(solution)/shard_map/cond/branch_0_fun/ppermute | solution.py:465
  279.8 24.9 %collective-permute-start.29 = (f32[6,256,256]{2,1,0:T(8,128)S(1)}, f32[6,256,256]{2,1,0:T(8,128)S(1)}, u32[]{:S(2)}, u32[]{:S(2)}) collective-permute-start(f32[6,256,256]{2,1,0:T(8,128)S(1)} %bitcast_dynamic-update-slice_fusion.refs_26_), channel_id=1, source_target_pairs={{24,0},{25,1},{26,2},{27,3}} | collective-permute-start | bytes 4718600 | tf_op jit(solution)/shard_map/cond/branch_0_fun/ppermute | solution.py:465
  290.7 14.1 %collective-permute-start.20 = (f32[3,256,256]{2,1,0:T(8,128)S(1)}, f32[3,256,256]{2,1,0:T(8,128)S(1)}, u32[]{:S(2)}, u32[]{:S(2)}) collective-permute-start(f32[3,256,256]{2,1,0:T(8,128)S(1)} %get-tuple-element.57), channel_id=1, source_target_pairs={{0,32},{4,228},{8,40},{12,236},{16,48},{20,244},{24,56},{28,252},{... | collective-permute-start | bytes 2359304 | tf_op jit(solution)/shard_map/cond/branch_0_fun/ppermute | solution.py:465
  300.8 28.5 %collective-permute-start.13 = (f32[6,256,256]{2,1,0:T(8,128)S(1)}, f32[6,256,256]{2,1,0:T(8,128)S(1)}, u32[]{:S(2)}, u32[]{:S(2)}) collective-permute-start(f32[6,256,256]{2,1,0:T(8,128)S(1)} %get-tuple-element.48), channel_id=1, source_target_pairs={{0,8},{4,28},{8,16},{12,4},{16,24},{20,12},{24,0},{28,20},{32,40},... | collective-permute-start | bytes 4718600 | tf_op jit(solution)/shard_map/cond/branch_0_fun/ppermute | solution.py:465
  301.0 39.2 %collective-permute-start.14 = (f32[6,256,256]{2,1,0:T(8,128)S(1)}, f32[6,256,256]{2,1,0:T(8,128)S(1)}, u32[]{:S(2)}, u32[]{:S(2)}) collective-permute-start(f32[6,256,256]{2,1,0:T(8,128)S(1)} %get-tuple-element.49), channel_id=1, source_target_pairs={{0,8},{4,28},{8,16},{12,4},{16,24},{20,12},{24,0},{28,20},{32,40},... | collective-permute-start | bytes 4718600 | tf_op jit(solution)/shard_map/cond/branch_0_fun/ppermute | solution.py:465
  303.4 39.6 %collective-permute-start.34 = (f32[6,256,256]{2,1,0:T(8,128)S(1)}, f32[6,256,256]{2,1,0:T(8,128)S(1)}, u32[]{:S(2)}, u32[]{:S(2)}) collective-permute-start(f32[6,256,256]{2,1,0:T(8,128)S(1)} %collective-permute-done.33), channel_id=1, source_target_pairs={{8,0},{9,1},{10,2},{11,3}} | collective-permute-start | bytes 4718600 | tf_op jit(solution)/shard_map/cond/branch_0_fun/ppermute | solution.py:465
  304.7 24.5 %collective-permute-start.19 = (f32[4,256,256]{2,1,0:T(8,128)S(1)}, f32[4,256,256]{2,1,0:T(8,128)S(1)}, u32[]{:S(2)}, u32[]{:S(2)}) collective-permute-start(f32[4,256,256]{2,1,0:T(8,128)S(1)} %get-tuple-element.56), channel_id=1, source_target_pairs={{0,32},{4,228},{8,40},{12,236},{16,48},{20,244},{24,56},{28,252},{... | collective-permute-start | bytes 3145736 | tf_op jit(solution)/shard_map/cond/branch_0_fun/ppermute | solution.py:465
  304.8 24.4 %collective-permute-start.21 = (f32[3,256,256]{2,1,0:T(8,128)S(1)}, f32[3,256,256]{2,1,0:T(8,128)S(1)}, u32[]{:S(2)}, u32[]{:S(2)}) collective-permute-start(f32[3,256,256]{2,1,0:T(8,128)S(1)} %get-tuple-element.58), channel_id=1, source_target_pairs={{0,32},{4,228},{8,40},{12,236},{16,48},{20,244},{24,56},{28,252},{... | collective-permute-start | bytes 2359304 | tf_op jit(solution)/shard_map/cond/branch_0_fun/ppermute | solution.py:465
  329.2 43.6 %collective-permute-start.39 = (f32[6,256,256]{2,1,0:T(8,128)S(1)}, f32[6,256,256]{2,1,0:T(8,128)S(1)}, u32[]{:S(2)}, u32[]{:S(2)}) collective-permute-start(f32[6,256,256]{2,1,0:T(8,128)S(1)} %collective-permute-done.13.refs_16_), channel_id=1, source_target_pairs={{0,8},{4,28},{8,16},{12,4},{16,24},{20,12},{24,0},{28,20},{32,40},... | collective-permute-start | bytes 4718600 | tf_op jit(solution)/shard_map/cond/branch_0_fun/ppermute | solution.py:465
  332.3 32.9 %collective-permute-start.30 = (f32[4,256,256]{2,1,0:T(8,128)S(1)}, f32[4,256,256]{2,1,0:T(8,128)S(1)}, u32[]{:S(2)}, u32[]{:S(2)}) collective-permute-start(f32[4,256,256]{2,1,0:T(8,128)S(1)} %collective-permute-done.19), channel_id=1, source_target_pairs={{0,32},{4,228},{8,40},{12,236},{16,48},{20,244},{24,56},{28,252},{... | collective-permute-start | bytes 3145736 | tf_op jit(solution)/shard_map/cond/branch_0_fun/ppermute | solution.py:465
  340.2 33.7 %collective-permute-start.40 = (f32[6,256,256]{2,1,0:T(8,128)S(1)}, f32[6,256,256]{2,1,0:T(8,128)S(1)}, u32[]{:S(2)}, u32[]{:S(2)}) collective-permute-start(f32[6,256,256]{2,1,0:T(8,128)S(1)} %collective-permute-done.14.refs_17_), channel_id=1, source_target_pairs={{0,8},{4,28},{8,16},{12,4},{16,24},{20,12},{24,0},{28,20},{32,40},... | collective-permute-start | bytes 4718600 | tf_op jit(solution)/shard_map/cond/branch_0_fun/ppermute | solution.py:465
  340.2 16.5 %collective-permute-start.31 = (f32[3,256,256]{2,1,0:T(8,128)S(1)}, f32[3,256,256]{2,1,0:T(8,128)S(1)}, u32[]{:S(2)}, u32[]{:S(2)}) collective-permute-start(f32[3,256,256]{2,1,0:T(8,128)S(1)} %collective-permute-done.20), channel_id=1, source_target_pairs={{0,32},{4,228},{8,40},{12,236},{16,48},{20,244},{24,56},{28,252},{... | collective-permute-start | bytes 2359304 | tf_op jit(solution)/shard_map/cond/branch_0_fun/ppermute | solution.py:465
  343.0 22.2 %collective-permute-start.32 = (f32[3,256,256]{2,1,0:T(8,128)S(1)}, f32[3,256,256]{2,1,0:T(8,128)S(1)}, u32[]{:S(2)}, u32[]{:S(2)}) collective-permute-start(f32[3,256,256]{2,1,0:T(8,128)S(1)} %collective-permute-done.21), channel_id=1, source_target_pairs={{0,32},{4,228},{8,40},{12,236},{16,48},{20,244},{24,56},{28,252},{... | collective-permute-start | bytes 2359304 | tf_op jit(solution)/shard_map/cond/branch_0_fun/ppermute | solution.py:465
  356.8 17.2 %collective-permute-start.44 = (f32[3,256,256]{2,1,0:T(8,128)S(1)}, f32[3,256,256]{2,1,0:T(8,128)S(1)}, u32[]{:S(2)}, u32[]{:S(2)}) collective-permute-start(f32[3,256,256]{2,1,0:T(8,128)S(1)} %collective-permute-done.31), channel_id=1, source_target_pairs={{0,32},{4,228},{8,40},{12,236},{16,48},{20,244},{24,56},{28,252},{... | collective-permute-start | bytes 2359304 | tf_op jit(solution)/shard_map/cond/branch_0_fun/ppermute | solution.py:465
  365.2 35.6 %collective-permute-start.35 = (f32[6,256,256]{2,1,0:T(8,128)S(1)}, f32[6,256,256]{2,1,0:T(8,128)S(1)}, u32[]{:S(2)}, u32[]{:S(2)}) collective-permute-start(f32[6,256,256]{2,1,0:T(8,128)S(1)} %get-tuple-element.69), channel_id=1, source_target_pairs={{0,8},{4,28},{8,16},{12,4},{16,24},{20,12},{24,0},{28,20},{32,40},... | collective-permute-start | bytes 4718600 | tf_op jit(solution)/shard_map/cond/branch_0_fun/ppermute | solution.py:465
  365.3 38.3 %collective-permute-start.36 = (f32[6,256,256]{2,1,0:T(8,128)S(1)}, f32[6,256,256]{2,1,0:T(8,128)S(1)}, u32[]{:S(2)}, u32[]{:S(2)}) collective-permute-start(f32[6,256,256]{2,1,0:T(8,128)S(1)} %collective-permute-done.13.refs_16_), channel_id=1, source_target_pairs={{0,4},{4,0},{8,12},{12,8},{16,20},{20,16},{24,28},{28,24},{32,36},... | collective-permute-start | bytes 4718600 | tf_op jit(solution)/shard_map/cond/branch_0_fun/ppermute | solution.py:465
  372.9 27.8 %collective-permute-start.43 = (f32[4,256,256]{2,1,0:T(8,128)S(1)}, f32[4,256,256]{2,1,0:T(8,128)S(1)}, u32[]{:S(2)}, u32[]{:S(2)}) collective-permute-start(f32[4,256,256]{2,1,0:T(8,128)S(1)} %collective-permute-done.30), channel_id=1, source_target_pairs={{0,32},{4,228},{8,40},{12,236},{16,48},{20,244},{24,56},{28,252},{... | collective-permute-start | bytes 3145736 | tf_op jit(solution)/shard_map/cond/branch_0_fun/ppermute | solution.py:465
  373.9 23.8 %collective-permute-start.45 = (f32[3,256,256]{2,1,0:T(8,128)S(1)}, f32[3,256,256]{2,1,0:T(8,128)S(1)}, u32[]{:S(2)}, u32[]{:S(2)}) collective-permute-start(f32[3,256,256]{2,1,0:T(8,128)S(1)} %collective-permute-done.32), channel_id=1, source_target_pairs={{0,32},{4,228},{8,40},{12,236},{16,48},{20,244},{24,56},{28,252},{... | collective-permute-start | bytes 2359304 | tf_op jit(solution)/shard_map/cond/branch_0_fun/ppermute | solution.py:465
  373.9 29.6 %collective-permute-start.37 = (f32[6,256,256]{2,1,0:T(8,128)S(1)}, f32[6,256,256]{2,1,0:T(8,128)S(1)}, u32[]{:S(2)}, u32[]{:S(2)}) collective-permute-start(f32[6,256,256]{2,1,0:T(8,128)S(1)} %collective-permute-done.14.refs_17_), channel_id=1, source_target_pairs={{0,4},{4,0},{8,12},{12,8},{16,20},{20,16},{24,28},{28,24},{32,36},... | collective-permute-start | bytes 4718600 | tf_op jit(solution)/shard_map/cond/branch_0_fun/ppermute | solution.py:465
  400.7 18.9 %collective-permute-start.42 = (f32[6,256,256]{2,1,0:T(8,128)S(1)}, f32[6,256,256]{2,1,0:T(8,128)S(1)}, u32[]{:S(2)}, u32[]{:S(2)}) collective-permute-start(f32[6,256,256]{2,1,0:T(8,128)S(1)} %collective-permute-done.40.refs_23_), channel_id=1, source_target_pairs={{0,4},{4,0},{8,12},{12,8},{16,20},{20,16},{24,28},{28,24},{32,36},... | collective-permute-start | bytes 4718600 | tf_op jit(solution)/shard_map/cond/branch_0_fun/ppermute | solution.py:465
  400.7 27.3 %collective-permute-start.38 = (f32[6,256,256]{2,1,0:T(8,128)S(1)}, f32[6,256,256]{2,1,0:T(8,128)S(1)}, u32[]{:S(2)}, u32[]{:S(2)}) collective-permute-start(f32[6,256,256]{2,1,0:T(8,128)S(1)} %collective-permute-done.35.refs_18_), channel_id=1, source_target_pairs={{0,4},{4,0},{8,12},{12,8},{16,20},{20,16},{24,28},{28,24},{32,36},... | collective-permute-start | bytes 4718600 | tf_op jit(solution)/shard_map/cond/branch_0_fun/ppermute | solution.py:465
  403.6 16.0 %collective-permute-start.49 = (f32[4,256,256]{2,1,0:T(8,128)S(1)}, f32[4,256,256]{2,1,0:T(8,128)S(1)}, u32[]{:S(2)}, u32[]{:S(2)}) collective-permute-start(f32[4,256,256]{2,1,0:T(8,128)S(1)} %collective-permute-done.43.refs_4_), channel_id=1, source_target_pairs={{0,32},{4,228},{8,40},{12,236},{16,48},{20,244},{24,56},{28,252},{... | collective-permute-start | bytes 3145736 | tf_op jit(solution)/shard_map/cond/branch_0_fun/ppermute | solution.py:465
  403.6 24.4 %collective-permute-start.50 = (f32[3,256,256]{2,1,0:T(8,128)S(1)}, f32[3,256,256]{2,1,0:T(8,128)S(1)}, u32[]{:S(2)}, u32[]{:S(2)}) collective-permute-start(f32[3,256,256]{2,1,0:T(8,128)S(1)} %collective-permute-done.44.refs_5_), channel_id=1, source_target_pairs={{0,32},{4,228},{8,40},{12,236},{16,48},{20,244},{24,56},{28,252},{... | collective-permute-start | bytes 2359304 | tf_op jit(solution)/shard_map/cond/branch_0_fun/ppermute | solution.py:465
  403.7 44.9 %collective-permute-start.46 = (f32[4,256,256]{2,1,0:T(8,128)S(1)}, f32[4,256,256]{2,1,0:T(8,128)S(1)}, u32[]{:S(2)}, u32[]{:S(2)}) collective-permute-start(f32[4,256,256]{2,1,0:T(8,128)S(1)} %collective-permute-done.43.refs_4_), channel_id=1, source_target_pairs={{0,4},{4,0},{8,12},{12,8},{16,20},{20,16},{24,28},{28,24},{32,36},... | collective-permute-start | bytes 3145736 | tf_op jit(solution)/shard_map/cond/branch_0_fun/ppermute | solution.py:465
  419.6 30.0 %collective-permute-start.51 = (f32[4,256,256]{2,1,0:T(8,128)S(1)}, f32[4,256,256]{2,1,0:T(8,128)S(1)}, u32[]{:S(2)}, u32[]{:S(2)}) collective-permute-start(f32[4,256,256]{2,1,0:T(8,128)S(1)} %collective-permute-done.49.refs_10_), channel_id=1, source_target_pairs={{0,4},{4,0},{8,12},{12,8},{16,20},{20,16},{24,28},{28,24},{32,36},... | collective-permute-start | bytes 3145736 | tf_op jit(solution)/shard_map/cond/branch_0_fun/ppermute | solution.py:465
  419.6 27.2 %collective-permute-start.47 = (f32[3,256,256]{2,1,0:T(8,128)S(1)}, f32[3,256,256]{2,1,0:T(8,128)S(1)}, u32[]{:S(2)}, u32[]{:S(2)}) collective-permute-start(f32[3,256,256]{2,1,0:T(8,128)S(1)} %collective-permute-done.44.refs_5_), channel_id=1, source_target_pairs={{0,4},{4,0},{8,12},{12,8},{16,20},{20,16},{24,28},{28,24},{32,36},... | collective-permute-start | bytes 2359304 | tf_op jit(solution)/shard_map/cond/branch_0_fun/ppermute | solution.py:465
  428.0 19.7 %collective-permute-start.48 = (f32[3,256,256]{2,1,0:T(8,128)S(1)}, f32[3,256,256]{2,1,0:T(8,128)S(1)}, u32[]{:S(2)}, u32[]{:S(2)}) collective-permute-start(f32[3,256,256]{2,1,0:T(8,128)S(1)} %collective-permute-done.45.refs_6_), channel_id=1, source_target_pairs={{0,4},{4,0},{8,12},{12,8},{16,20},{20,16},{24,28},{28,24},{32,36},... | collective-permute-start | bytes 2359304 | tf_op jit(solution)/shard_map/cond/branch_0_fun/ppermute | solution.py:465
  428.0 20.6 %collective-permute-start.52 = (f32[3,256,256]{2,1,0:T(8,128)S(1)}, f32[3,256,256]{2,1,0:T(8,128)S(1)}, u32[]{:S(2)}, u32[]{:S(2)}) collective-permute-start(f32[3,256,256]{2,1,0:T(8,128)S(1)} %collective-permute-done.50.refs_11_), channel_id=1, source_target_pairs={{0,4},{4,0},{8,12},{12,8},{16,20},{20,16},{24,28},{28,24},{32,36},... | collective-permute-start | bytes 2359304 | tf_op jit(solution)/shard_map/cond/branch_0_fun/ppermute | solution.py:465
  (44 other events, 957.1 us)
